TPU v7x, 128 devices: a whole 4x4x4 slice. The times are simulated.
128 devices in a mesh: prow: 16 (over y_hi, z, core), pcol: 8 (over x, y_lo).
Axes of the slice: x: 4, y: 4 (y_hi: 2, y_lo: 2; y = y_hi * 2 + y_lo), z: 4, core: 2. Of those that a mesh axis runs over, the one named last changes fastest.
Arguments:
- prior: float32 [32, 256, 32, 256], P('prow', None, 'pcol'), may hold values from -1 to 6, as said below
- lfac: float32 [32, 256, 32, 256], P('prow', None, 'pcol'), may hold values from -0.03125 to 0.03125
- tile_mask: int32 [32, 32], replicated, may hold values 0 or 1
- dinv: float32 [4, 256, 256], replicated, may hold values from -1 to 4, as said below
Outputs:
- inverse: float32 [32, 256, 32, 256], P('prow', None, 'pcol')
Inputs may be any that keep to these rules, and one draw needn't show every extreme that they name: `prior`: symmetric as a 8192 x 8192 matrix in global order. `dinv`: each block is symmetric.
All inputs are finite; a program needn't handle non-finite values.
Results may differ from a plain program's by a relative error of at most 0.0001.
Values sent between devices are 32-bit elements; how exact they have to be, the bound alone decides.
A program may use at most 64 MiB of HBM per device.

v0:
```python
import jax
import jax.numpy as jnp
from jax import lax
from jax.sharding import PartitionSpec as P


def from_root(value, axis, source):
    kept = jnp.where(lax.axis_index(axis) == source, value, 0).astype(value.dtype)
    return lax.psum(kept, axis)


def column_live(tile_mask, glob_rows, step, tiles):
    column = lax.dynamic_index_in_dim(tile_mask, step, 1, keepdims=False)
    picked = jnp.sum(
        (jnp.arange(tiles)[None, :] == glob_rows[:, None]).astype(jnp.int32) * column[None, :],
        axis=1,
    )
    return (picked * (glob_rows > step).astype(jnp.int32)).astype(jnp.float32)


def body(prior, lfac, tile_mask, dinv):
    rows_n = lax.axis_size("prow")
    cols_n = lax.axis_size("pcol")
    rank_r = lax.axis_index("prow")
    rank_c = lax.axis_index("pcol")
    tile_rows, width, tile_cols, _ = prior.shape
    tiles = tile_rows * rows_n
    steps = dinv.shape[0]
    ratio = rows_n // cols_n
    glob_rows = jnp.arange(tile_rows, dtype=jnp.int32) * rows_n + rank_r
    glob_cols = jnp.arange(tile_cols, dtype=jnp.int32) * cols_n + rank_c

    def advance(turn, inverse):
        step = steps - 1 - turn
        live = column_live(tile_mask, glob_rows, step, tiles)
        local = (
            lax.dynamic_index_in_dim(lfac, step // cols_n, 2, keepdims=False) * live[:, None, None]
        )
        panel = from_root(local, "pcol", step % cols_n)
        partial_value = -jnp.einsum(
            "apbq,apr->bqr",
            inverse,
            panel,
            precision=lax.Precision.HIGHEST,
            preferred_element_type=jnp.float32,
        )
        column_block = lax.psum(partial_value, "prow")
        grouped = column_block.reshape(tile_rows, ratio, width, width)
        mine = lax.dynamic_index_in_dim(grouped, rank_r // cols_n, 1, keepdims=False)
        row_index = step // rows_n
        old_row = lax.dynamic_index_in_dim(inverse, row_index, 0, keepdims=False)
        new_row = jnp.transpose(column_block, (2, 0, 1))
        row_flag = (rank_r == step % rows_n) & (glob_cols > step)
        inverse = lax.dynamic_update_index_in_dim(
            inverse, jnp.where(row_flag[None, :, None], new_row, old_row), row_index, 0
        )
        row_values = from_root(mine, "pcol", rank_r % cols_n)
        partial_diag = jnp.einsum(
            "apr,apq->rq",
            panel,
            row_values,
            precision=lax.Precision.HIGHEST,
            preferred_element_type=jnp.float32,
        )
        diag = lax.dynamic_index_in_dim(dinv, step, 0, keepdims=False) - lax.psum(
            partial_diag, "prow"
        )
        col_index = step // cols_n
        old_col = lax.dynamic_index_in_dim(inverse, col_index, 2, keepdims=False)
        col_flag = (rank_c == step % cols_n) & (glob_rows > step)
        new_col = jnp.where(col_flag[:, None, None], row_values, old_col)
        diag_flag = (
            (rank_c == step % cols_n)
            & (rank_r == step % rows_n)
            & (jnp.arange(tile_rows) == row_index)
        )
        new_col = jnp.where(diag_flag[:, None, None], diag[None], new_col)
        return lax.dynamic_update_index_in_dim(inverse, new_col, col_index, 2)

    return lax.fori_loop(0, steps, advance, prior)


def solution(mesh):
    placed = (P("prow", None, "pcol", None), P("prow", None, "pcol", None), P(), P())
    return jax.shard_map(
        body, mesh=mesh, in_specs=placed, out_specs=P("prow", None, "pcol", None), check_vma=False
    )
```

profile of v0, /device:TPU:32, one launch (start us, length us, event | category | flops | bytes accessed | tf_op | source)
XLA Modules:
  0.0 1784.2 jit_solution(11828817813894326076)
XLA Ops:
  6.5 2.0 copy.13
  8.6 1766.3 %while.19 = (s32[]{:T(128)}, f32[2,256,4,256]{3,1,0,2:T(8,128)S(1)}, s32[]{:T(128)}, f32[2,256,4,256]{3,2,1,0:T(4,128)}, s32[32,32]{0,1:T(8,128)S(1)}, /*index=5...) while((s32[]{:T(128)}, ...), condition=%wide.region_6.7_spmd.clone.clone, body=%wide.region_0.6_spmd.clone.clone.sunk | while | flops 2015101184 | bytes 36440956 | solution.py:80
  8.7 2.1 constant_dynamic-slice_fusion.10
  12.4 76.8 %all-reduce.5.cloned.1.call-done = f32[2,256,256]{1,2,0:T(8,128)} async-done(((f32[2,256,256]{1,2,0:T(8,128)}), f32[2,256,256]{1,2,0:T(8,128)}) %all-reduce.5.cloned.1.call-update) | async-done | bytes 524304 | tf_op jit(solution)/shard_map/while/body/eval_jaxpr/psum | solution.py:9
  89.2 3.9 fusion.32
  93.2 135.0 %all-reduce.7.cloned.1.call-done = f32[4,256,256]{1,2,0:T(8,128)} async-done(((f32[4,256,256]{1,2,0:T(8,128)}), f32[4,256,256]{1,2,0:T(8,128)}) %all-reduce.7.cloned.1.call-update) | async-done | bytes 1048592 | tf_op jit(solution)/shard_map/while/body/eval_jaxpr/psum | solution.py:47
  230.6 80.6 %all-reduce.9.cloned.1.call-done = f32[2,256,256]{2,1,0:T(8,128)} async-done(((f32[2,256,256]{2,1,0:T(8,128)}), f32[2,256,256]{2,1,0:T(8,128)}) %all-reduce.9.cloned.1.call-update) | async-done | bytes 524304 | tf_op jit(solution)/shard_map/while/body/eval_jaxpr/psum | solution.py:9
  311.2 2.5 convolution_bitcast_fusion.3
  313.7 1.4 bitcast_dynamic-update-slice_fusion.4
  315.2 130.9 %all-reduce.11.cloned.1.call-done = f32[256,256]{1,0:T(8,128)} async-done(((f32[256,256]{1,0:T(8,128)}), f32[256,256]{1,0:T(8,128)}) %all-reduce.11.cloned.1.call-update) | async-done | bytes 262160 | tf_op jit(solution)/shard_map/while/body/eval_jaxpr/psum | solution.py:65
  447.5 2.1 constant_dynamic-slice_fusion.10
  451.2 80.6 %all-reduce.5.cloned.1.call-done = f32[2,256,256]{1,2,0:T(8,128)} async-done(((f32[2,256,256]{1,2,0:T(8,128)}), f32[2,256,256]{1,2,0:T(8,128)}) %all-reduce.5.cloned.1.call-update) | async-done | bytes 524304 | tf_op jit(solution)/shard_map/while/body/eval_jaxpr/psum | solution.py:9
  531.8 3.9 fusion.32
  535.8 135.0 %all-reduce.7.cloned.1.call-done = f32[4,256,256]{1,2,0:T(8,128)} async-done(((f32[4,256,256]{1,2,0:T(8,128)}), f32[4,256,256]{1,2,0:T(8,128)}) %all-reduce.7.cloned.1.call-update) | async-done | bytes 1048592 | tf_op jit(solution)/shard_map/while/body/eval_jaxpr/psum | solution.py:47
  673.2 80.7 %all-reduce.9.cloned.1.call-done = f32[2,256,256]{2,1,0:T(8,128)} async-done(((f32[2,256,256]{2,1,0:T(8,128)}), f32[2,256,256]{2,1,0:T(8,128)}) %all-reduce.9.cloned.1.call-update) | async-done | bytes 524304 | tf_op jit(solution)/shard_map/while/body/eval_jaxpr/psum | solution.py:9
  753.9 2.5 convolution_bitcast_fusion.3
  757.9 130.7 %all-reduce.11.cloned.1.call-done = f32[256,256]{1,0:T(8,128)} async-done(((f32[256,256]{1,0:T(8,128)}), f32[256,256]{1,0:T(8,128)}) %all-reduce.11.cloned.1.call-update) | async-done | bytes 262160 | tf_op jit(solution)/shard_map/while/body/eval_jaxpr/psum | solution.py:65
  889.9 2.1 constant_dynamic-slice_fusion.10
  893.7 80.6 %all-reduce.5.cloned.1.call-done = f32[2,256,256]{1,2,0:T(8,128)} async-done(((f32[2,256,256]{1,2,0:T(8,128)}), f32[2,256,256]{1,2,0:T(8,128)}) %all-reduce.5.cloned.1.call-update) | async-done | bytes 524304 | tf_op jit(solution)/shard_map/while/body/eval_jaxpr/psum | solution.py:9
  974.3 3.9 fusion.32
  978.3 135.0 %all-reduce.7.cloned.1.call-done = f32[4,256,256]{1,2,0:T(8,128)} async-done(((f32[4,256,256]{1,2,0:T(8,128)}), f32[4,256,256]{1,2,0:T(8,128)}) %all-reduce.7.cloned.1.call-update) | async-done | bytes 1048592 | tf_op jit(solution)/shard_map/while/body/eval_jaxpr/psum | solution.py:47
  1115.6 80.6 %all-reduce.9.cloned.1.call-done = f32[2,256,256]{2,1,0:T(8,128)} async-done(((f32[2,256,256]{2,1,0:T(8,128)}), f32[2,256,256]{2,1,0:T(8,128)}) %all-reduce.9.cloned.1.call-update) | async-done | bytes 524304 | tf_op jit(solution)/shard_map/while/body/eval_jaxpr/psum | solution.py:9
  1196.3 2.5 convolution_bitcast_fusion.3
  1200.3 130.9 %all-reduce.11.cloned.1.call-done = f32[256,256]{1,0:T(8,128)} async-done(((f32[256,256]{1,0:T(8,128)}), f32[256,256]{1,0:T(8,128)}) %all-reduce.11.cloned.1.call-update) | async-done | bytes 262160 | tf_op jit(solution)/shard_map/while/body/eval_jaxpr/psum | solution.py:65
  1332.6 2.1 constant_dynamic-slice_fusion.10
  1336.3 80.6 %all-reduce.5.cloned.1.call-done = f32[2,256,256]{1,2,0:T(8,128)} async-done(((f32[2,256,256]{1,2,0:T(8,128)}), f32[2,256,256]{1,2,0:T(8,128)}) %all-reduce.5.cloned.1.call-update) | async-done | bytes 524304 | tf_op jit(solution)/shard_map/while/body/eval_jaxpr/psum | solution.py:9
  1416.9 3.9 fusion.32
  1420.9 135.0 %all-reduce.7.cloned.1.call-done = f32[4,256,256]{1,2,0:T(8,128)} async-done(((f32[4,256,256]{1,2,0:T(8,128)}), f32[4,256,256]{1,2,0:T(8,128)}) %all-reduce.7.cloned.1.call-update) | async-done | bytes 1048592 | tf_op jit(solution)/shard_map/while/body/eval_jaxpr/psum | solution.py:47
  1558.3 80.5 %all-reduce.9.cloned.1.call-done = f32[2,256,256]{2,1,0:T(8,128)} async-done(((f32[2,256,256]{2,1,0:T(8,128)}), f32[2,256,256]{2,1,0:T(8,128)}) %all-reduce.9.cloned.1.call-update) | async-done | bytes 524304 | tf_op jit(solution)/shard_map/while/body/eval_jaxpr/psum | solution.py:9
  1638.8 2.5 convolution_bitcast_fusion.3
  1642.8 130.9 %all-reduce.11.cloned.1.call-done = f32[256,256]{1,0:T(8,128)} async-done(((f32[256,256]{1,0:T(8,128)}), f32[256,256]{1,0:T(8,128)}) %all-reduce.11.cloned.1.call-update) | async-done | bytes 262160 | tf_op jit(solution)/shard_map/while/body/eval_jaxpr/psum | solution.py:65
  1775.0 2.7 copy.16
  (110 shorter events, 25.0 us)
Async XLA Ops:
  6.5 2.0 copy-start.1
  8.6 80.6 %all-reduce.5.cloned.1.call-start = ((), (), s32[]{:S(2)}) async-start(), calls=%async_computation | async-start | bytes 1048576 | tf_op jit(solution)/shard_map/while/body/eval_jaxpr/psum | solution.py:9
  12.4 215.8 %all-reduce.7.cloned.1.call-start = ((), (), s32[]{:S(2)}) async-start(), calls=%async_computation.1 | async-start | bytes 2097152 | tf_op jit(solution)/shard_map/while/body/eval_jaxpr/psum | solution.py:47
  93.1 218.1 %all-reduce.9.cloned.1.call-start = ((), (), s32[]{:S(2)}) async-start(), calls=%async_computation.2 | async-start | bytes 1048576 | tf_op jit(solution)/shard_map/while/body/eval_jaxpr/psum | solution.py:9
  230.3 215.8 %all-reduce.11.cloned.1.call-start = ((), (), s32[]{:S(2)}) async-start(), calls=%async_computation.3 | async-start | bytes 524288 | tf_op jit(solution)/shard_map/while/body/eval_jaxpr/psum | solution.py:65
  315.2 132.1 %copy-start = (f32[2,256,256]{2,1,0:T(8,128)S(1)}, f32[2,256,256]{2,1,0:T(8,128)}, u32[]{:S(2)}) copy-start(f32[2,256,256]{2,1,0:T(8,128)} %all-reduce.9.cloned.1.call-done) | copy-start | bytes 1572868 | tf_op jit(solution)/shard_map/while
  447.4 84.4 %all-reduce.5.cloned.1.call-start = ((), (), s32[]{:S(2)}) async-start(), calls=%async_computation | async-start | bytes 1048576 | tf_op jit(solution)/shard_map/while/body/eval_jaxpr/psum | solution.py:9
  451.2 219.7 %all-reduce.7.cloned.1.call-start = ((), (), s32[]{:S(2)}) async-start(), calls=%async_computation.1 | async-start | bytes 2097152 | tf_op jit(solution)/shard_map/while/body/eval_jaxpr/psum | solution.py:47
  535.7 218.1 %all-reduce.9.cloned.1.call-start = ((), (), s32[]{:S(2)}) async-start(), calls=%async_computation.2 | async-start | bytes 1048576 | tf_op jit(solution)/shard_map/while/body/eval_jaxpr/psum | solution.py:9
  673.0 215.7 %all-reduce.11.cloned.1.call-start = ((), (), s32[]{:S(2)}) async-start(), calls=%async_computation.3 | async-start | bytes 524288 | tf_op jit(solution)/shard_map/while/body/eval_jaxpr/psum | solution.py:65
  757.8 131.9 %copy-start = (f32[2,256,256]{2,1,0:T(8,128)S(1)}, f32[2,256,256]{2,1,0:T(8,128)}, u32[]{:S(2)}) copy-start(f32[2,256,256]{2,1,0:T(8,128)} %all-reduce.9.cloned.1.call-done) | copy-start | bytes 1572868 | tf_op jit(solution)/shard_map/while
  889.9 84.4 %all-reduce.5.cloned.1.call-start = ((), (), s32[]{:S(2)}) async-start(), calls=%async_computation | async-start | bytes 1048576 | tf_op jit(solution)/shard_map/while/body/eval_jaxpr/psum | solution.py:9
  893.6 219.7 %all-reduce.7.cloned.1.call-start = ((), (), s32[]{:S(2)}) async-start(), calls=%async_computation.1 | async-start | bytes 2097152 | tf_op jit(solution)/shard_map/while/body/eval_jaxpr/psum | solution.py:47
  978.2 218.1 %all-reduce.9.cloned.1.call-start = ((), (), s32[]{:S(2)}) async-start(), calls=%async_computation.2 | async-start | bytes 1048576 | tf_op jit(solution)/shard_map/while/body/eval_jaxpr/psum | solution.py:9
  1115.4 215.8 %all-reduce.11.cloned.1.call-start = ((), (), s32[]{:S(2)}) async-start(), calls=%async_computation.3 | async-start | bytes 524288 | tf_op jit(solution)/shard_map/while/body/eval_jaxpr/psum | solution.py:65
  1200.2 132.1 %copy-start = (f32[2,256,256]{2,1,0:T(8,128)S(1)}, f32[2,256,256]{2,1,0:T(8,128)}, u32[]{:S(2)}) copy-start(f32[2,256,256]{2,1,0:T(8,128)} %all-reduce.9.cloned.1.call-done) | copy-start | bytes 1572868 | tf_op jit(solution)/shard_map/while
  1332.5 84.4 %all-reduce.5.cloned.1.call-start = ((), (), s32[]{:S(2)}) async-start(), calls=%async_computation | async-start | bytes 1048576 | tf_op jit(solution)/shard_map/while/body/eval_jaxpr/psum | solution.py:9
  1336.2 219.7 %all-reduce.7.cloned.1.call-start = ((), (), s32[]{:S(2)}) async-start(), calls=%async_computation.1 | async-start | bytes 2097152 | tf_op jit(solution)/shard_map/while/body/eval_jaxpr/psum | solution.py:47
  1420.8 218.0 %all-reduce.9.cloned.1.call-start = ((), (), s32[]{:S(2)}) async-start(), calls=%async_computation.2 | async-start | bytes 1048576 | tf_op jit(solution)/shard_map/while/body/eval_jaxpr/psum | solution.py:9
  1558.0 215.7 %all-reduce.11.cloned.1.call-start = ((), (), s32[]{:S(2)}) async-start(), calls=%async_computation.3 | async-start | bytes 524288 | tf_op jit(solution)/shard_map/while/body/eval_jaxpr/psum | solution.py:65
  1642.7 132.1 %copy-start = (f32[2,256,256]{2,1,0:T(8,128)S(1)}, f32[2,256,256]{2,1,0:T(8,128)}, u32[]{:S(2)}) copy-start(f32[2,256,256]{2,1,0:T(8,128)} %all-reduce.9.cloned.1.call-done) | copy-start | bytes 1572868 | tf_op jit(solution)/shard_map/while
Sparse Core Ops, SparseCore 0:
  12.5 76.6 all-reduce.4
  93.2 134.8 all-reduce.6
  230.7 80.4 all-reduce.8
  313.9 132.2 all-reduce.10
  451.3 80.4 all-reduce.4
  535.9 134.8 all-reduce.6
  673.3 80.5 all-reduce.8
  756.5 132.0 all-reduce.10
  893.7 80.4 all-reduce.4
  978.3 134.8 all-reduce.6
  1115.8 80.4 all-reduce.8
  1198.9 132.2 all-reduce.10
  1336.4 80.4 all-reduce.4
  1421.0 134.8 all-reduce.6
  1558.2 80.5 all-reduce.8
  1641.4 132.2 all-reduce.10
where the time goes:
time: 1790 us; the launch traced here: 1780 us
  waiting for transfers between devices  1700 us (95%)
  matrix products  25.6 us (1%)
  local copies, waits for them, and re-layouts  20.3 us (1%)
  other arithmetic  18.4 us (1%)
    psum x8, waiting for transfers between devices, from_root(): return lax.psum(kept, axis)  641 us
    psum x4, waiting for transfers between devices, advance(): column_block = lax.psum(partial_value, 'prow')  540 us
    psum x4, waiting for transfers between devices, advance(): lax.psum(partial_diag, 'prow')  524 us
  transfers between devices with their start and end apart: 16, of which 16 were waited for; matrix products, arithmetic and copies ran while one was open for 0% of the time, Pallas kernels for 0%

commit v1 on v0

v1 whole, which is shorter than its diff:
```python
import jax
import jax.numpy as jnp
from jax import lax
from jax.experimental import pallas as pl
from jax.experimental.pallas import tpu as pltpu
from jax.sharding import PartitionSpec as P

B = 256
S = 4
F32 = jnp.float32
BF16 = jnp.bfloat16
MESH = pl.DeviceIdType.MESH
LOW = [(1, 0), (2, 0), (2, 1), (3, 0), (3, 1), (3, 2)]
CORE_OF = {1: 1, 2: 0, 3: 1}


def split(value):
    hi = value.astype(BF16)
    lo = (value - hi.astype(F32)).astype(BF16)
    return hi, lo


def dot3(a, b, dims=((1,), (0,))):
    def one(left, right):
        return lax.dot_general(left, right, (dims, ((), ())), preferred_element_type=F32)

    return one(a[0], b[0]) + (one(a[0], b[1]) + one(a[1], b[0]))


def kernel(prior, lfac, mask, dinv, out,
           g32, gh, gl, lt32, pt, ph, plo, lt, ut, cr, op, om, rm, rp, yr, xt, xa, xb, xo, xh, xl,
           zp, zc, zr, zs, zf, mt, dv, zo,
           g_sem, l_sem, d_sem, o_sem, w_sem,
           s_out, r_out, s_x, r_x, s_y, r_y,
           s_l, r_l, s_c, r_c, s_zo, r_zo, s_zr, r_zr, s_yh, r_yh,
           s_xa, r_xa, s_xb, r_xb, s_zc, r_zc, s_zd, r_zd, s_zf, r_zf):
    row = lax.axis_index("prow")
    col = lax.axis_index("pcol")
    yh, z, core = row // 8, (row // 2) % 4, row % 2
    x, yl = col // 2, col % 2
    quad = row // 2

    def at(r=None, c=None):
        return {"prow": row if r is None else r, "pcol": col if c is None else c}

    def remote(src, dst, ssem, rsem, where):
        return pltpu.make_async_remote_copy(
            src_ref=src, dst_ref=dst, send_sem=ssem, recv_sem=rsem, device_id=where, device_id_type=MESH)

    c_x = (x + 1 - 2 * (x % 2)) * 2 + yl
    c_y = x * 2 + 1 - yl
    c_o = (3 - x) * 2 + yl
    r_core = row + 1 - 2 * core
    r_zp = yh * 8 + ((z + 1) % 4) * 2 + core
    r_zm = yh * 8 + ((z + 3) % 4) * 2 + core
    r_y2 = (row + 8) % 16
    b_row, b_col = col + 8 * yh, z
    b_self = (b_row == row) & (b_col == col)
    a_self = z == row

    loads = []
    for a in range(2):
        for b in range(4):
            loads.append(pltpu.make_async_copy(prior.at[a, :, b, :], g32.at[b, pl.ds(a * B, B), :], g_sem.at[a, b]))
    keep = pltpu.make_async_copy(prior, out, o_sem)
    ltile = [pltpu.make_async_copy(lfac.at[a, :, 0, :], lt32.at[a], l_sem.at[a]) for a in range(2)]
    dload = pltpu.make_async_copy(dinv, dv, d_sem)

    @pl.when(col < S)
    def _():
        for copy in ltile:
            copy.start()
    for copy in loads:
        copy.start()
    dload.start()
    keep.start()

    barrier = pltpu.get_barrier_semaphore()

    def greet(where):
        pl.semaphore_signal(barrier, inc=1, device_id=where, device_id_type=MESH)

    for step in range(1, 16):
        greet(at(r=(row + step) % 16))
    for c in (c_x, c_y, c_o):
        greet(at(c=c))
    greet(at(r=r_y2, c=c_y))

    def b_source(a):
        return (row // 8) * 8 + col * 2 + a, row % 8

    for a in range(2):
        sr, sc = b_source(a)

        @pl.when((col < S) & jnp.logical_not((sr == row) & (sc == col)))
        def _():
            greet(at(r=sr, c=sc))

    @pl.when(col < S)
    def _():
        for a in range(2):
            ltile[a].wait()
            live = mask[row + 16 * a, col] * (row + 16 * a > col).astype(jnp.int32)
            pt[col, a] = lt32[a].T * live.astype(F32)

    pl.semaphore_wait(barrier, 19 + jnp.where(b_self, 0, 1))

    near = jnp.where((x == 0) | (x == 3), 0, 1)
    k_p, k_s = 2 * near + yl, 2 * (1 - near) + yl
    k_pd, k_sd = 2 * near + 1 - yl, 2 * (1 - near) + 1 - yl

    c_out = [remote(pt.at[k_p, a], pt.at[k_p, a], s_out.at[a], r_out.at[a], at(c=c_o)) for a in range(2)]
    c_xs = [remote(pt.at[k_p, a], pt.at[k_p, a], s_x.at[a], r_x.at[a], at(c=c_x)) for a in range(2)]
    c_ys = [remote(pt.at[k_p, a], pt.at[k_p, a], s_y.at[a], r_y.at[a], at(c=c_y)) for a in range(2)]
    c_xd = remote(pt.at[k_pd, 0], pt.at[k_pd, 0], s_x.at[2], r_x.at[2], at(c=c_x))
    c_yd = remote(pt.at[k_s, 1], pt.at[k_s, 1], s_y.at[2], r_y.at[2], at(c=c_y))
    w_xs = [remote(pt.at[k_s, a], pt.at[k_s, a], s_x.at[a], r_x.at[a], at(c=c_x)) for a in range(2)]
    w_ys = [remote(pt.at[k_pd, a], pt.at[k_pd, a], s_y.at[a], r_y.at[a], at(c=c_y)) for a in range(2)]
    w_xd = remote(pt.at[k_sd, 0], pt.at[k_sd, 0], s_x.at[2], r_x.at[2], at(c=c_x))
    w_yd = remote(pt.at[k_sd, 1], pt.at[k_sd, 1], s_y.at[2], r_y.at[2], at(c=c_y))

    for a in range(2):
        @pl.when(x < 2)
        def _():
            c_out[a].start()

        @pl.when(x >= 2)
        def _():
            c_out[a].wait_recv()
        c_xs[a].start()
        c_ys[a].start()

    for a in range(2):
        for b in range(4):
            loads[a * 4 + b].wait()
    for b in range(4):
        hi, lo = split(g32[b])
        gh[b] = hi
        gl[b] = lo

    w_ys[0].wait_recv()
    c_xd.start()
    w_xs[0].wait_recv()
    w_xs[1].wait_recv()
    c_yd.start()
    w_ys[1].wait_recv()
    w_xd.wait_recv()
    w_yd.wait_recv()

    def l_copy(u, slot, where):
        return remote(lt.at[u], lt.at[u], s_l.at[u, slot], r_l.at[u], where)

    def l_wait(u):
        l_copy(u, 0, at(r=r_core)).wait_recv()

    def l_routes(u, j):
        routes = [(row >= 0, l_copy(u, 0, at(r=r_core))), (yh == 0, l_copy(u, 1, at(r=r_y2, c=c_y)))]
        if j == 1:
            routes.append((row == 1, l_copy(u, 2, at(r=r_zp))))
            routes.append(((row == 1) | (row == 7), l_copy(u, 3, at(r=r_zm))))
        else:
            routes.append(((row == j) | (row == j + 2), l_copy(u, 2, at(r=r_zp))))
            routes.append((row == j, l_copy(u, 3, at(r=r_zm))))
        return routes

    order = {0: [(2, 1), (2, 0)], 1: [(3, 2), (3, 1), (1, 0), (3, 0)]}
    for own in range(2):
        @pl.when(core == own)
        def _():
            for j, k in order[own]:
                u = LOW.index((j, k))

                @pl.when(row == j)
                def _():
                    lt[u] = pt[k, 0]

                @pl.when(row != j)
                def _():
                    l_wait(u)
                for cond, copy in l_routes(u, j):
                    @pl.when(cond)
                    def _():
                        copy.start()

    zero = jnp.where(row < S, 0.0, 1.0).astype(F32)
    c_core = []
    for k in (3, 2, 1, 0):
        acc = jnp.concatenate([pt[k, 0] * zero, pt[k, 1]], axis=1)
        for j in range(k + 1, S):
            u = LOW.index((j, k))

            @pl.when(core != CORE_OF[j])
            def _():
                l_wait(u)
            acc = acc - dot3(split(lt[u]), (ph[j], plo[j]))
        hi, lo = split(acc)
        ph[k] = hi
        plo[k] = lo

        @pl.loop(0, 4)
        def _(t):
            ut[k, t] = dot3((ph[k], plo[k]), (gh[t], gl[t]))
        copy = remote(ut.at[k, pl.ds(2 - 2 * core, 2)], cr.at[k], s_c.at[k], r_c.at[k], at(r=r_core))
        copy.start()
        c_core.append(copy)

    c_opp = [remote(ut.at[(z + 2) % 4, 2 * core], op, s_zo.at[0], r_zo.at[0], at(r=r_zp)),
             remote(ut.at[(z + 2) % 4, 2 * core + 1], om, s_zo.at[1], r_zo.at[1], at(r=r_zm))]
    c_rm = [remote(ut.at[(z + 1) % 4, 2 * core + u], rm.at[u], s_zr.at[u], r_zr.at[u], at(r=r_zp)) for u in range(2)]
    c_rp = [remote(ut.at[(z + 3) % 4, 2 * core + u], rp.at[u], s_zr.at[2 + u], r_zr.at[2 + u], at(r=r_zm))
            for u in range(2)]
    for n, k in enumerate((3, 2, 1, 0)):
        c_core[n].wait_recv()
        for u in range(2):
            ut[k, 2 * core + u] = ut[k, 2 * core + u] + cr[k, u]
        rel = (k - z + 4) % 4

        @pl.when(rel == 2)
        def _():
            c_opp[0].start()
            c_opp[1].start()

        @pl.when(rel == 1)
        def _():
            c_rm[1].start()

        @pl.when(rel == 3)
        def _():
            c_rp[0].start()
    c_opp[0].wait_recv()
    ut[(z + 1) % 4, 2 * core] = ut[(z + 1) % 4, 2 * core] + op[...]
    c_rm[0].start()
    c_opp[1].wait_recv()
    ut[(z + 3) % 4, 2 * core + 1] = ut[(z + 3) % 4, 2 * core + 1] + om[...]
    c_rp[1].start()
    for u in (1, 0):
        c_rm[u].wait_recv()
    for u in (0, 1):
        c_rp[u].wait_recv()
    away = 1 - yh
    ut[z, 2 * core + away] = ut[z, 2 * core + away] + (rm[away] + rp[away])
    c_yh = remote(ut.at[z, 2 * core + away], yr, s_yh, r_yh, at(r=r_y2))
    c_yh.start()
    mine = ut[z, 2 * core + yh] + (rm[yh] + rp[yh])
    c_yh.wait_recv()
    xt[...] = -(mine + yr[...])

    t_own = 2 * core + yh
    c_xa = remote(xt, xa.at[t_own], s_xa, r_xa.at[t_own], at(r=z))
    c_xb = remote(xt, xb.at[core], s_xb, r_xb.at[core], at(r=b_row, c=b_col))

    @pl.when(jnp.logical_not(b_self))
    def _():
        c_xb.start()

    @pl.when(b_self)
    def _():
        xb[core] = xt[...]

    @pl.when(jnp.logical_not(a_self))
    def _():
        c_xa.start()

    @pl.when(a_self)
    def _():
        xa[t_own] = xt[...]

    dload.wait()

    @pl.when((row < S) & (col < S))
    def _():
        ones = (lax.broadcasted_iota(jnp.int32, (B, B), 0) == lax.broadcasted_iota(jnp.int32, (B, B), 1))
        for k in range(S):
            for m in range(S):
                if m < k:
                    mt[k, m] = jnp.zeros((B, B), F32)
                elif m == k:
                    mt[k, m] = ones.astype(F32)
                else:
                    acc = lt[LOW.index((m, k))]
                    for j in range(k + 1, m):
                        acc = acc + dot3(split(mt[k, j]), split(lt[LOW.index((m, j))]))
                    mt[k, m] = -acc
        zo[...] = jnp.zeros((B, B), F32)
        for m in range(S):
            half = dot3(split(mt[row, m]), split(dv[m]))
            zo[...] = zo[...] + dot3(split(half), split(mt[col, m]), ((1,), (1,)))

    c_zc = remote(zp.at[1 - core], zc, s_zc, r_zc, at(r=r_core))
    c_zd = [remote(zp.at[core, :, pl.ds(((quad + d) % 8) * 32, 32), :], zr.at[d - 1], s_zd.at[d - 1], r_zd.at[d - 1],
                   at(r=((quad + d) % 8) * 2 + core)) for d in range(1, 8)]
    c_zf = [remote(zs.at[m], zf.at[pl.ds(quad * 32, 32), :], s_zf.at[m], r_zf.at[quad], at(r=2 * m + core))
            for m in range(2)]

    @pl.when(col < S)
    def _():
        for a in range(2):
            sr, sc = b_source(a)

            @pl.when(jnp.logical_not((sr == row) & (sc == col)))
            def _():
                remote(xt, xb.at[a], s_xb, r_xb.at[a], at(r=b_row, c=b_col)).wait_recv()
            xo[a] = xb[a].T
            hi, lo = split(xo[a])
            xh[pl.ds(a * B, B), :] = hi
            xl[pl.ds(a * B, B), :] = lo
        for l in range(S):
            zp[l % 2, l // 2] = dot3((ph[l], plo[l]), (xh[...], xl[...]))
        c_zc.start()
        c_zc.wait_recv()
        zp[core] = zp[core] + zc[...]
        for copy in c_zd:
            copy.start()
        acc = zp[core, :, pl.ds(quad * 32, 32), :]
        for d in range(7):
            c_zd[d].wait_recv()
            acc = acc + zr[d]
        zs[...] = acc
        for m in range(2):
            @pl.when(quad != m)
            def _():
                c_zf[m].start()

            @pl.when(quad == m)
            def _():
                zf[pl.ds(quad * 32, 32), :] = zs[m]

        @pl.when(row < S)
        def _():
            for q in range(8):
                @pl.when(quad != q)
                def _():
                    remote(zs.at[0], zf.at[pl.ds(q * 32, 32), :], s_zf.at[0], r_zf.at[q], at(r=r_core)).wait_recv()
            zo[...] = zo[...] - zf[...]

    keep.wait()
    w_row = [pltpu.make_async_copy(xa.at[t], out.at[0, :, t, :], w_sem.at[t]) for t in range(4)]
    w_col = [pltpu.make_async_copy(xo.at[a], out.at[a, :, 0, :], w_sem.at[4 + a]) for a in range(2)]
    w_dia = pltpu.make_async_copy(zo, out.at[0, :, 0, :], w_sem.at[6])
    writes = [((row < S) & (col >= S), w_row[0])] + [(row < S, w_row[t]) for t in range(1, 4)]
    writes += [((col < S) & (row >= S), w_col[0]), (col < S, w_col[1]), ((row < S) & (col < S), w_dia)]

    @pl.when(row < S)
    def _():
        for t in range(4):
            @pl.when(jnp.logical_not(a_self & (t_own == t)))
            def _():
                remote(xt, xa.at[t], s_xa, r_xa.at[t], at(r=r_core)).wait_recv()
    for cond, copy in writes:
        @pl.when(cond)
        def _():
            copy.start()

    @pl.when(x < 2)
    def _():
        for copy in c_out:
            copy.wait_send()
    for copy in c_xs + c_ys + [c_xd, c_yd] + c_core + c_opp + c_rm + c_rp + [c_yh]:
        copy.wait_send()
    for own in range(2):
        @pl.when(core == own)
        def _():
            for j, k in order[own]:
                for cond, copy in l_routes(LOW.index((j, k)), j):
                    @pl.when(cond)
                    def _():
                        copy.wait_send()

    @pl.when(jnp.logical_not(b_self))
    def _():
        c_xb.wait_send()

    @pl.when(jnp.logical_not(a_self))
    def _():
        c_xa.wait_send()

    @pl.when(col < S)
    def _():
        c_zc.wait_send()
        for copy in c_zd:
            copy.wait_send()
        for m in range(2):
            @pl.when(quad != m)
            def _():
                c_zf[m].wait_send()
    for cond, copy in writes:
        @pl.when(cond)
        def _():
            copy.wait()


def body(prior, lfac, tile_mask, dinv):
    def vmem(*shape, kind=F32):
        return pltpu.VMEM(shape, kind)

    dma = pltpu.SemaphoreType.DMA
    scratch = [
        vmem(4, 2 * B, B), vmem(4, 2 * B, B, kind=BF16), vmem(4, 2 * B, B, kind=BF16),
        vmem(2, B, B), vmem(4, 2, B, B), vmem(4, B, 2 * B, kind=BF16), vmem(4, B, 2 * B, kind=BF16),
        vmem(6, B, B), vmem(4, 4, B, B), vmem(4, 2, B, B),
        vmem(B, B), vmem(B, B), vmem(2, B, B), vmem(2, B, B), vmem(B, B),
        vmem(B, B), vmem(4, B, B), vmem(2, B, B), vmem(2, B, B),
        vmem(2 * B, B, kind=BF16), vmem(2 * B, B, kind=BF16),
        vmem(2, 2, B, B), vmem(2, B, B), vmem(7, 2, 32, B), vmem(2, 32, B), vmem(B, B),
        vmem(4, 4, B, B), vmem(4, B, B), vmem(B, B),
        dma((2, 4)), dma((2,)), dma, dma, dma((7,)),
        dma((2,)), dma((2,)), dma((3,)), dma((3,)), dma((3,)), dma((3,)),
        dma((6, 4)), dma((6,)), dma((4,)), dma((4,)), dma((2,)), dma((2,)), dma((4,)), dma((4,)), dma, dma,
        dma, dma((4,)), dma, dma((2,)), dma, dma, dma((7,)), dma((7,)), dma((2,)), dma((8,)),
    ]
    return pl.pallas_call(
        kernel,
        out_shape=jax.ShapeDtypeStruct(prior.shape, F32),
        in_specs=[pl.BlockSpec(memory_space=pl.ANY), pl.BlockSpec(memory_space=pl.ANY),
                  pl.BlockSpec(memory_space=pltpu.SMEM), pl.BlockSpec(memory_space=pl.ANY)],
        out_specs=pl.BlockSpec(memory_space=pl.ANY),
        scratch_shapes=scratch,
        compiler_params=pltpu.CompilerParams(
            collective_id=0, has_side_effects=True, vmem_limit_bytes=56 * 1024 * 1024),
    )(prior, lfac, tile_mask, dinv)


def solution(mesh):
    placed = (P("prow", None, "pcol", None), P("prow", None, "pcol", None), P(), P())
    return jax.shard_map(
        body, mesh=mesh, in_specs=placed, out_specs=P("prow", None, "pcol", None), check_vma=False
    )
```

time: 1790 us -> 149 us (0.08)
  waiting for transfers between devices: 1700 us -> 0 us
  Pallas kernels: 0 us -> 143 us
  matrix products: 25.6 us -> 0 us
  other arithmetic: 18.4 us -> 0 us
    psum x16 -> x0, waiting for transfers between devices: 1700 us -> none  [the longest x8 641 us: from_root(): return lax.psum(kept, axis)]
    pallas_call x0 -> x1, Pallas kernels: none -> 143 us  [body(): pl.pallas_call(kernel, out_shape=jax.ShapeDtypeStruct(prior.shape, F32),...]
    dot_general x8 -> x0, matrix products: 25.6 us -> none  [the longest x4 15.6 us: advance(): jnp.einsum('apbq,apr->bqr', inverse, panel, precision=lax.Precision.HIGHE...]
  transfers between devices with their start and end apart: 16 -> 0, of which waited for: 16 -> 0; matrix products, arithmetic and copies ran while one was open for 0% -> 0% of each run, Pallas kernels for 0% -> 0%
where the time goes in v1:
time: 149 us; the launch traced here: 146 us
  Pallas kernels  143 us (96%)
  local copies, waits for them, and re-layouts  3.27 us (2%)
    pallas_call x1, Pallas kernels, body(): pl.pallas_call(kernel, out_shape=jax.ShapeDtypeStruct(prior.shape, F32),...  143 us
    unnamed x1, local copies, waits for them, and re-layouts  3.27 us

profile of v1, /device:TPU:32, one launch (start us, length us, event | category | flops | bytes accessed | tf_op | source)
XLA Modules:
  0.0 146.2 jit_solution(3909913019139247874)
XLA Ops:
  0.0 143.0 %shard_map.46 = f32[2,256,4,256]{3,2,1,0:T(4,128)} custom-call(f32[2,256,4,256]{3,2,1,0:T(4,128)} %prior.1, f32[2,256,4,256]{3,2,1,0:T(4,128)} %lfac.1, s32[32,32]{1,0:T(8,128)} %mask.1, f32[4,256,256]{2,1,0:T(8,128)} %dinv.1), custom_call_target="tpu_custom_call" | custom-call | tf_op jit(solution)/shard_map/pallas_call | solution.py:411
  143.0 3.3 %copy.6 = f32[2,256,4,256]{3,2,1,0:T(4,128)} copy(f32[2,256,4,256]{3,2,1,0:T(4,128)} %shard_map.46) | data formatting | bytes 4194304

commit v2 on v1

v2 whole, which is shorter than its diff:
```python
import jax
import jax.numpy as jnp
from jax import lax
from jax.experimental import pallas as pl
from jax.experimental.pallas import tpu as pltpu
from jax.sharding import PartitionSpec as P

B = 256
S = 4
F32 = jnp.float32
BF16 = jnp.bfloat16
MESH = pl.DeviceIdType.MESH
LOW = [(1, 0), (2, 0), (2, 1), (3, 0), (3, 1), (3, 2)]
CORE_OF = {1: 1, 2: 0, 3: 1}


def split(value):
    hi = value.astype(BF16)
    lo = (value - hi.astype(F32)).astype(BF16)
    return hi, lo


def dot3(a, b, dims=((1,), (0,))):
    def one(left, right):
        return lax.dot_general(left, right, (dims, ((), ())), preferred_element_type=F32)

    return one(a[0], b[0]) + (one(a[0], b[1]) + one(a[1], b[0]))


def kernel(prior, lfac, mask, dinv, out,
           g32, gh, gl, lt32, pt, ph, plo, lt, ut, cr, op, om, rm, rp, yr, xt, xa, xb, xo, xh, xl,
           zp, zc, zr, zs, zf, mt, dv, zo,
           g_sem, l_sem, d_sem, o_sem, w_sem,
           s_out, r_out, s_x, r_x, s_y, r_y,
           s_l, r_l, s_c, r_c, s_zo, r_zo, s_zr, r_zr, s_yh, r_yh,
           s_xa, r_xa, s_xb, r_xb, s_zc, r_zc, s_zd, r_zd, s_zf, r_zf):
    row = lax.axis_index("prow")
    col = lax.axis_index("pcol")
    yh, z, core = row // 8, (row // 2) % 4, row % 2
    x, yl = col // 2, col % 2
    quad = row // 2

    def at(r=None, c=None):
        return {"prow": row if r is None else r, "pcol": col if c is None else c}

    def remote(src, dst, ssem, rsem, where):
        return pltpu.make_async_remote_copy(
            src_ref=src, dst_ref=dst, send_sem=ssem, recv_sem=rsem, device_id=where, device_id_type=MESH)

    c_x = (x + 1 - 2 * (x % 2)) * 2 + yl
    c_y = x * 2 + 1 - yl
    c_o = (3 - x) * 2 + yl
    r_core = row + 1 - 2 * core
    r_zp = yh * 8 + ((z + 1) % 4) * 2 + core
    r_zm = yh * 8 + ((z + 3) % 4) * 2 + core
    r_y2 = (row + 8) % 16
    b_row, b_col = col + 8 * yh, (z - x + 4) % 4
    b_self = (b_row == row) & (b_col == col)
    a_self = row == b_col

    loads = []
    for a in range(2):
        for b in range(4):
            loads.append(pltpu.make_async_copy(prior.at[a, :, b, :], g32.at[b, pl.ds(a * B, B), :], g_sem.at[a, b]))
    keeps = []
    for a in range(2):
        for b in range(4):
            stays = row >= 0
            if a == 0:
                stays = stays & (row >= S)
            if b == 0:
                stays = stays & (col >= S)
            keeps.append((stays, pltpu.make_async_copy(
                g32.at[b, pl.ds(a * B, B), :], out.at[a, :, b, :], o_sem.at[a, b])))
    ltile = [pltpu.make_async_copy(lfac.at[a, :, 0, :], lt32.at[a], l_sem.at[a]) for a in range(2)]
    dload = pltpu.make_async_copy(dinv, dv, d_sem)

    @pl.when(col < S)
    def _():
        for copy in ltile:
            copy.start()
    for copy in loads:
        copy.start()
    dload.start()

    barrier = pltpu.get_barrier_semaphore()

    def greet(where):
        pl.semaphore_signal(barrier, inc=1, device_id=where, device_id_type=MESH)

    for step in range(1, 16):
        greet(at(r=(row + step) % 16))
    for c in (c_x, c_y, c_o):
        greet(at(c=c))
    greet(at(r=r_y2, c=c_y))

    def b_source(a):
        return yh * 8 + (z + col) % 4 * 2 + a, row % 8

    for a in range(2):
        sr, sc = b_source(a)

        @pl.when((col < S) & jnp.logical_not((sr == row) & (sc == col)))
        def _():
            greet(at(r=sr, c=sc))

    @pl.when(col < S)
    def _():
        for a in range(2):
            ltile[a].wait()
            live = mask[row + 16 * a, col] * (row + 16 * a > col).astype(jnp.int32)
            turned = lt32[a].T * live.astype(F32)
            pt[col, 2 * a] = turned[:B // 2]
            pt[col, 2 * a + 1] = turned[B // 2:]

    pl.semaphore_wait(barrier, 19 + jnp.where(b_self, 0, 1))

    near = jnp.where((x == 0) | (x == 3), 0, 1)
    k_p, k_s = 2 * near + yl, 2 * (1 - near) + yl
    k_pd, k_sd = 2 * near + 1 - yl, 2 * (1 - near) + 1 - yl

    def quarter(k, ch, ssem, rsem, where):
        return remote(pt.at[k, ch], pt.at[k, ch], ssem, rsem, where)

    source, inner = x < 2, x >= 2
    always = row >= 0
    to_x, to_y, to_o = at(c=c_x), at(c=c_y), at(c=c_o)

    def out_recv(ch):
        quarter(k_p, ch, s_out.at[ch], r_out.at[ch], to_o).wait_recv()

    def x_recv(ch):
        quarter(k_s, ch, s_x.at[ch], r_x.at[ch], to_x).wait_recv()

    def y_recv(ch):
        quarter(k_pd, ch, s_y.at[ch], r_y.at[ch], to_y).wait_recv()

    def xd_recv(ch):
        quarter(k_sd, ch, s_x.at[4 + ch], r_x.at[4 + ch], to_x).wait_recv()

    def yd_recv(ch):
        quarter(k_sd, ch, s_y.at[4 + ch], r_y.at[4 + ch], to_y).wait_recv()

    def l_copy(u, slot, where):
        return remote(lt.at[u], lt.at[u], s_l.at[u, slot], r_l.at[u], where)

    def l_wait(u):
        l_copy(u, 0, at(r=r_core)).wait_recv()

    def l_routes(u, j):
        routes = [(always, l_copy(u, 0, at(r=r_core))), (yh == 0, l_copy(u, 1, at(r=r_y2, c=c_y)))]
        if j == 1:
            routes.append((row == 1, l_copy(u, 2, at(r=r_zp))))
            routes.append(((row == 1) | (row == 7), l_copy(u, 3, at(r=r_zm))))
        else:
            routes.append(((row == j) | (row == j + 2), l_copy(u, 2, at(r=r_zp))))
            routes.append((row == j, l_copy(u, 3, at(r=r_zm))))
        return routes

    def l_step(k, first, half_y=0):
        for j in (2, 3, 1):
            u = (j * (j - 1)) // 2 + k
            here = (core == CORE_OF[j]) & (k < j)

            @pl.when(here & (row == j) if first else here & (row != j) & (yh == half_y))
            def _():
                if first:
                    lt[u, pl.ds(0, B // 2), :] = pt[k, 0]
                    lt[u, pl.ds(B // 2, B // 2), :] = pt[k, 1]
                else:
                    l_wait(u)
                for cond, copy in l_routes(u, j):
                    @pl.when(cond)
                    def _():
                        copy.start()

    @pl.when(source)
    def _():
        for ch in range(4):
            quarter(k_p, ch, s_out.at[ch], r_out.at[ch], to_o).start()
            quarter(k_p, ch, s_x.at[ch], r_x.at[ch], to_x).start()
            quarter(k_p, ch, s_y.at[ch], r_y.at[ch], to_y).start()
        l_step(k_p, True)

    for a in range(2):
        for b in range(4):
            loads[a * 4 + b].wait()
            cond, copy = keeps[a * 4 + b]

            @pl.when(cond)
            def _():
                copy.start()
    for b in range(4):
        hi, lo = split(g32[b])
        gh[b] = hi
        gl[b] = lo

    @pl.when(source)
    def _():
        y_recv(0)
        quarter(k_pd, 0, s_x.at[4], r_x.at[4], to_x).start()
        y_recv(1)
        quarter(k_pd, 1, s_x.at[5], r_x.at[5], to_x).start()
        l_step(k_pd, True)
        x_recv(0)
        x_recv(1)
        l_step(k_s, True)

    @pl.when(inner)
    def _():
        for ch in range(2):
            out_recv(ch)
            quarter(k_p, ch, s_x.at[ch], r_x.at[ch], to_x).start()
            quarter(k_p, ch, s_y.at[ch], r_y.at[ch], to_y).start()
        l_step(k_p, True)
        y_recv(0)
        quarter(k_pd, 0, s_x.at[4], r_x.at[4], to_x).start()
        out_recv(2)
        quarter(k_p, 2, s_x.at[2], r_x.at[2], to_x).start()
        y_recv(1)
        l_step(k_pd, True)

    @pl.when(source)
    def _():
        y_recv(2)
        quarter(k_pd, 2, s_out.at[4], r_out.at[4], to_o).start()
        x_recv(2)
        quarter(k_s, 2, s_y.at[6], r_y.at[6], to_y).start()
        y_recv(3)
        quarter(k_pd, 3, s_out.at[5], r_out.at[5], to_o).start()
        x_recv(3)
        quarter(k_s, 3, s_y.at[7], r_y.at[7], to_y).start()

    @pl.when(inner)
    def _():
        x_recv(0)
        x_recv(1)
        quarter(k_s, 1, s_y.at[5], r_y.at[5], to_y).start()
        l_step(k_s, True)
        out_recv(3)
        quarter(k_p, 3, s_x.at[3], r_x.at[3], to_x).start()
        x_recv(2)
        quarter(k_s, 2, s_y.at[6], r_y.at[6], to_y).start()
        x_recv(3)
        quarter(k_s, 3, s_y.at[7], r_y.at[7], to_y).start()
    l_step(k_p, False)
    xd_recv(0)

    @pl.when(source)
    def _():
        xd_recv(1)

    @pl.when(inner)
    def _():
        yd_recv(1)
    l_step(k_sd, True)
    l_step(k_pd, False)
    yd_recv(2)
    yd_recv(3)

    @pl.when(inner)
    def _():
        for ch in (2, 3):
            quarter(k_pd, ch, s_out.at[2 + ch], r_out.at[2 + ch], to_o).wait_recv()
    l_step(k_s, False)
    l_step(k_sd, False)
    for k in (k_pd, k_p, k_sd, k_s):
        l_step(k, False, 1)

    zero = jnp.where(row < S, 0.0, 1.0).astype(F32)
    half = B // 2
    c_core = {k: remote(ut.at[k, pl.ds(2 - 2 * core, 2)], cr.at[k], s_c.at[k], r_c.at[k], at(r=r_core))
              for k in range(S)}

    def products(k):
        acc = jnp.concatenate(
            [jnp.concatenate([pt[k, h] * zero, pt[k, 2 + h]], axis=1) for h in range(2)], axis=0)
        for j in range(k + 1, S):
            u = LOW.index((j, k))

            @pl.when(core != CORE_OF[j])
            def _():
                l_wait(u)
            acc = acc - dot3(split(lt[u]), (ph[j], plo[j]))
        hi, lo = split(acc)
        ph[k] = hi
        plo[k] = lo

        @pl.loop(0, 4)
        def _(t):
            ut[k, t] = dot3((ph[k], plo[k]), (gh[t], gl[t]))
        c_core[k].start()

    k_own = (z - x + 4) % 4
    k_op, k_rm, k_rp = (k_own + 2) % 4, (k_own + 1) % 4, (k_own + 3) % 4
    halves = [pl.ds(0, half), pl.ds(half, half)]

    def unit(k, u, h):
        return ut.at[k, 2 * core + u, halves[h], :]

    c_op = [remote(unit(k_op, 0, h), op.at[h], s_zo.at[0, h], r_zo.at[0, h], at(r=r_zp)) for h in range(2)]
    c_om = [remote(unit(k_op, 1, h), om.at[h], s_zo.at[1, h], r_zo.at[1, h], at(r=r_zm)) for h in range(2)]
    c_rm = [[remote(unit(k_rm, u, h), rm.at[u, h], s_zr.at[0, u, h], r_zr.at[0, u, h], at(r=r_zp)) for h in range(2)]
            for u in range(2)]
    c_rp = [[remote(unit(k_rp, u, h), rp.at[u, h], s_zr.at[1, u, h], r_zr.at[1, u, h], at(r=r_zm)) for h in range(2)]
            for u in range(2)]

    def core_sum(k):
        c_core[k].wait_recv()
        for u in range(2):
            ut[k, 2 * core + u] = ut[k, 2 * core + u] + cr[k, u]

        @pl.when(k == k_op)
        def _():
            for h in range(2):
                c_op[h].start()
                c_om[h].start()

        @pl.when(k == k_rm)
        def _():
            for h in range(2):
                c_rm[1][h].start()

        @pl.when(k == k_rp)
        def _():
            for h in range(2):
                c_rp[0][h].start()

    products(3)
    products(2)
    core_sum(3)
    products(1)
    core_sum(2)
    products(0)
    core_sum(1)
    core_sum(0)
    for h in range(2):
        c_op[h].wait_recv()
        ut[k_rm, 2 * core, halves[h], :] = ut[k_rm, 2 * core, halves[h], :] + op[h]
        c_rm[0][h].start()
        c_om[h].wait_recv()
        ut[k_rp, 2 * core + 1, halves[h], :] = ut[k_rp, 2 * core + 1, halves[h], :] + om[h]
        c_rp[1][h].start()
    away = 1 - yh
    c_yh = [remote(unit(k_own, away, h), yr.at[h], s_yh.at[h], r_yh.at[h], at(r=r_y2)) for h in range(2)]
    for h in range(2):
        for u in range(2):
            c_rm[u][h].wait_recv()
            c_rp[u][h].wait_recv()
        ut[k_own, 2 * core + away, halves[h], :] = (
            ut[k_own, 2 * core + away, halves[h], :] + (rm[away, h] + rp[away, h]))
        c_yh[h].start()

    t_own = 2 * core + yh
    c_xa = [remote(xt.at[h], xa.at[t_own, halves[h], :], s_xa.at[h], r_xa.at[t_own, h], at(r=k_own)) for h in range(2)]
    c_xb = [remote(xt.at[h], xb.at[core, halves[h], :], s_xb.at[h], r_xb.at[core, h], at(r=b_row, c=b_col))
            for h in range(2)]
    for h in range(2):
        mine = ut[k_own, 2 * core + yh, halves[h], :] + (rm[yh, h] + rp[yh, h])
        c_yh[h].wait_recv()
        xt[h] = -(mine + yr[h])

        @pl.when(jnp.logical_not(b_self))
        def _():
            c_xb[h].start()

        @pl.when(b_self)
        def _():
            xb[core, halves[h], :] = xt[h]
    for h in range(2):
        @pl.when(jnp.logical_not(a_self))
        def _():
            c_xa[h].start()

        @pl.when(a_self)
        def _():
            xa[t_own, halves[h], :] = xt[h]

    dload.wait()

    @pl.when((row < S) & (col < S))
    def _():
        ones = (lax.broadcasted_iota(jnp.int32, (B, B), 0) == lax.broadcasted_iota(jnp.int32, (B, B), 1))
        for k in range(S):
            for m in range(S):
                if m < k:
                    mt[k, m] = jnp.zeros((B, B), F32)
                elif m == k:
                    mt[k, m] = ones.astype(F32)
                else:
                    acc = lt[LOW.index((m, k))]
                    for j in range(k + 1, m):
                        acc = acc + dot3(split(mt[k, j]), split(lt[LOW.index((m, j))]))
                    mt[k, m] = -acc
        zo[...] = jnp.zeros((B, B), F32)
        for m in range(S):
            part = dot3(split(mt[row, m]), split(dv[m]))
            zo[...] = zo[...] + dot3(split(part), split(mt[col, m]), ((1,), (1,)))

    c_zc = remote(zp.at[1 - core], zc, s_zc, r_zc, at(r=r_core))
    c_zd = [remote(zp.at[core, :, pl.ds(((quad + d) % 8) * 32, 32), :], zr.at[d - 1], s_zd.at[d - 1], r_zd.at[d - 1],
                   at(r=((quad + d) % 8) * 2 + core)) for d in range(1, 8)]
    c_zf = [remote(zs.at[m], zf.at[pl.ds(quad * 32, 32), :], s_zf.at[m], r_zf.at[quad], at(r=2 * m + core))
            for m in range(2)]

    @pl.when(col < S)
    def _():
        for a in range(2):
            sr, sc = b_source(a)

            @pl.when(jnp.logical_not((sr == row) & (sc == col)))
            def _():
                for h in range(2):
                    remote(xt.at[h], xb.at[a, halves[h], :], s_xb.at[h], r_xb.at[a, h], at(r=b_row, c=b_col)).wait_recv()
            xo[a] = xb[a].T
            hi, lo = split(xo[a])
            xh[pl.ds(a * B, B), :] = hi
            xl[pl.ds(a * B, B), :] = lo
        for l in range(S):
            zp[l % 2, l // 2] = dot3((ph[l], plo[l]), (xh[...], xl[...]))
        c_zc.start()
        c_zc.wait_recv()
        zp[core] = zp[core] + zc[...]
        for copy in c_zd:
            copy.start()
        acc = zp[core, :, pl.ds(quad * 32, 32), :]
        for d in range(7):
            c_zd[d].wait_recv()
            acc = acc + zr[d]
        zs[...] = acc
        for m in range(2):
            @pl.when(quad != m)
            def _():
                c_zf[m].start()

            @pl.when(quad == m)
            def _():
                zf[pl.ds(quad * 32, 32), :] = zs[m]

        @pl.when(row < S)
        def _():
            for q in range(8):
                @pl.when(quad != q)
                def _():
                    remote(zs.at[0], zf.at[pl.ds(q * 32, 32), :], s_zf.at[0], r_zf.at[q], at(r=r_core)).wait_recv()
            zo[...] = zo[...] - zf[...]

    w_row = [pltpu.make_async_copy(xa.at[t], out.at[0, :, t, :], w_sem.at[t]) for t in range(4)]
    w_col = [pltpu.make_async_copy(xo.at[a], out.at[a, :, 0, :], w_sem.at[4 + a]) for a in range(2)]
    w_dia = pltpu.make_async_copy(zo, out.at[0, :, 0, :], w_sem.at[6])
    writes = [((row < S) & (col >= S), w_row[0])] + [(row < S, w_row[t]) for t in range(1, 4)]
    writes += [((col < S) & (row >= S), w_col[0]), (col < S, w_col[1]), ((row < S) & (col < S), w_dia)]

    @pl.when(row < S)
    def _():
        for t in range(4):
            @pl.when(jnp.logical_not(a_self & (t_own == t)))
            def _():
                for h in range(2):
                    remote(xt.at[h], xa.at[t, halves[h], :], s_xa.at[h], r_xa.at[t, h], at(r=r_core)).wait_recv()
    for cond, copy in writes:
        @pl.when(cond)
        def _():
            copy.start()

    @pl.when(source)
    def _():
        for ch in range(4):
            quarter(k_p, ch, s_out.at[ch], r_out.at[ch], to_o).wait_send()
        for ch in (2, 3):
            quarter(k_pd, ch, s_out.at[2 + ch], r_out.at[2 + ch], to_o).wait_send()
            quarter(k_p, ch, s_y.at[ch], r_y.at[ch], to_y).wait_send()
        quarter(k_pd, 1, s_x.at[5], r_x.at[5], to_x).wait_send()

    @pl.when(inner)
    def _():
        quarter(k_s, 1, s_y.at[5], r_y.at[5], to_y).wait_send()
    for ch in range(4):
        quarter(k_p, ch, s_x.at[ch], r_x.at[ch], to_x).wait_send()
    for ch in range(2):
        quarter(k_p, ch, s_y.at[ch], r_y.at[ch], to_y).wait_send()
    quarter(k_pd, 0, s_x.at[4], r_x.at[4], to_x).wait_send()
    for ch in (2, 3):
        quarter(k_s, ch, s_y.at[4 + ch], r_y.at[4 + ch], to_y).wait_send()
    for j, k in LOW:
        @pl.when(core == CORE_OF[j])
        def _():
            for cond, copy in l_routes(LOW.index((j, k)), j):
                @pl.when(cond)
                def _():
                    copy.wait_send()
    for copy in list(c_core.values()) + c_op + c_om + c_rm[0] + c_rm[1] + c_rp[0] + c_rp[1] + c_yh:
        copy.wait_send()

    @pl.when(jnp.logical_not(b_self))
    def _():
        for copy in c_xb:
            copy.wait_send()

    @pl.when(jnp.logical_not(a_self))
    def _():
        for copy in c_xa:
            copy.wait_send()

    @pl.when(col < S)
    def _():
        c_zc.wait_send()
        for copy in c_zd:
            copy.wait_send()
        for m in range(2):
            @pl.when(quad != m)
            def _():
                c_zf[m].wait_send()
    for cond, copy in writes + keeps:
        @pl.when(cond)
        def _():
            copy.wait()


def body(prior, lfac, tile_mask, dinv):
    def vmem(*shape, kind=F32):
        return pltpu.VMEM(shape, kind)

    dma = pltpu.SemaphoreType.DMA
    hb = B // 2
    scratch = [
        vmem(4, 2 * B, B), vmem(4, 2 * B, B, kind=BF16), vmem(4, 2 * B, B, kind=BF16),
        vmem(2, B, B), vmem(4, 4, hb, B), vmem(4, B, 2 * B, kind=BF16), vmem(4, B, 2 * B, kind=BF16),
        vmem(6, B, B), vmem(4, 4, B, B), vmem(4, 2, B, B),
        vmem(2, hb, B), vmem(2, hb, B), vmem(2, 2, hb, B), vmem(2, 2, hb, B), vmem(2, hb, B),
        vmem(2, hb, B), vmem(4, B, B), vmem(2, B, B), vmem(2, B, B),
        vmem(2 * B, B, kind=BF16), vmem(2 * B, B, kind=BF16),
        vmem(2, 2, B, B), vmem(2, B, B), vmem(7, 2, 32, B), vmem(2, 32, B), vmem(B, B),
        vmem(4, 4, B, B), vmem(4, B, B), vmem(B, B),
        dma((2, 4)), dma((2,)), dma, dma((2, 4)), dma((7,)),
        dma((6,)), dma((6,)), dma((6,)), dma((6,)), dma((8,)), dma((8,)),
        dma((6, 4)), dma((6,)), dma((4,)), dma((4,)),
        dma((2, 2)), dma((2, 2)), dma((2, 2, 2)), dma((2, 2, 2)), dma((2,)), dma((2,)),
        dma((2,)), dma((4, 2)), dma((2,)), dma((2, 2)),
        dma, dma, dma((7,)), dma((7,)), dma((2,)), dma((8,)),
    ]
    return pl.pallas_call(
        kernel,
        out_shape=jax.ShapeDtypeStruct(prior.shape, F32),
        in_specs=[pl.BlockSpec(memory_space=pl.ANY), pl.BlockSpec(memory_space=pl.ANY),
                  pl.BlockSpec(memory_space=pltpu.SMEM), pl.BlockSpec(memory_space=pl.ANY)],
        out_specs=pl.BlockSpec(memory_space=pl.ANY),
        scratch_shapes=scratch,
        compiler_params=pltpu.CompilerParams(
            collective_id=0, has_side_effects=True, vmem_limit_bytes=56 * 1024 * 1024),
    )(prior, lfac, tile_mask, dinv)


def solution(mesh):
    placed = (P("prow", None, "pcol", None), P("prow", None, "pcol", None), P(), P())
    return jax.shard_map(
        body, mesh=mesh, in_specs=placed, out_specs=P("prow", None, "pcol", None), check_vma=False
    )
```

time: 149 us -> 126 us (0.85)
  the two profiles are of different devices: /device:TPU:32 before, /device:TPU:3 now
where the time goes in v2:
time: 126 us; the launch traced here: 125 us
  Pallas kernels  122 us (97%)
  local copies, waits for them, and re-layouts  3.27 us (3%)
    pallas_call x1, Pallas kernels, body(): pl.pallas_call(kernel, out_shape=jax.ShapeDtypeStruct(prior.shape, F32),...  122 us
    unnamed x1, local copies, waits for them, and re-layouts  3.27 us

profile of v2, /device:TPU:3, one launch (start us, length us, event | category | flops | bytes accessed | tf_op | source)
XLA Modules:
  0.0 125.5 jit_solution(10266495443396236399)
XLA Ops:
  0.0 122.2 %shard_map.46 = f32[2,256,4,256]{3,2,1,0:T(4,128)} custom-call(f32[2,256,4,256]{3,2,1,0:T(4,128)} %prior.1, f32[2,256,4,256]{3,2,1,0:T(4,128)} %lfac.1, s32[32,32]{1,0:T(8,128)} %mask.1, f32[4,256,256]{2,1,0:T(8,128)} %dinv.1), custom_call_target="tpu_custom_call" | custom-call | tf_op jit(solution)/shard_map/pallas_call | solution.py:542
  122.2 3.3 %copy.6 = f32[2,256,4,256]{3,2,1,0:T(4,128)} copy(f32[2,256,4,256]{3,2,1,0:T(4,128)} %shard_map.46) | data formatting | bytes 4194304

commit v3 on v2

v3 whole, which is shorter than its diff:
```python
import jax
import jax.numpy as jnp
from jax import lax
from jax.experimental import pallas as pl
from jax.experimental.pallas import tpu as pltpu
from jax.sharding import PartitionSpec as P

B = 256
S = 4
F32 = jnp.float32
BF16 = jnp.bfloat16
MESH = pl.DeviceIdType.MESH
LOW = [(1, 0), (2, 0), (2, 1), (3, 0), (3, 1), (3, 2)]
CORE_OF = {1: 1, 2: 0, 3: 1}


def split(value):
    hi = value.astype(BF16)
    lo = (value - hi.astype(F32)).astype(BF16)
    return hi, lo


def dot3(a, b, dims=((1,), (0,))):
    def one(left, right):
        return lax.dot_general(left, right, (dims, ((), ())), preferred_element_type=F32)

    return one(a[0], b[0]) + (one(a[0], b[1]) + one(a[1], b[0]))


def kernel(prior, lfac, mask, dinv, out,
           g32, gth, gtl, lt32, pn, pbh, pbl, ph, plo, lt, lbh, lbl, ut, cr, op, om, rm, rp, yr, xt, xa, xb, xat, xh, xl,
           zp, zc, zr, zs, zf, mt, dv, zo,
           g_sem, l_sem, d_sem, o_sem, w_sem,
           s_out, r_out, s_x, r_x, s_y, r_y,
           s_l, r_l, s_c, r_c, s_zo, r_zo, s_zr, r_zr, s_yh, r_yh,
           s_xa, r_xa, s_xb, r_xb, s_zc, r_zc, s_zd, r_zd, s_zf, r_zf):
    row = lax.axis_index("prow")
    col = lax.axis_index("pcol")
    yh, z, core = row // 8, (row // 2) % 4, row % 2
    x, yl = col // 2, col % 2
    quad = row // 2

    def at(r=None, c=None):
        return {"prow": row if r is None else r, "pcol": col if c is None else c}

    def remote(src, dst, ssem, rsem, where):
        return pltpu.make_async_remote_copy(
            src_ref=src, dst_ref=dst, send_sem=ssem, recv_sem=rsem, device_id=where, device_id_type=MESH)

    c_x = (x + 1 - 2 * (x % 2)) * 2 + yl
    c_y = x * 2 + 1 - yl
    c_o = (3 - x) * 2 + yl
    r_core = row + 1 - 2 * core
    r_zp = yh * 8 + ((z + 1) % 4) * 2 + core
    r_zm = yh * 8 + ((z + 3) % 4) * 2 + core
    r_y2 = (row + 8) % 16
    t_own = 2 * core + yh
    b_row = col + 8 * yh
    q_own = pl.ds(64 * z, 64)

    loads = []
    for a in range(2):
        for b in range(4):
            loads.append(pltpu.make_async_copy(prior.at[a, :, b, :], g32.at[b, pl.ds(a * B, B), :], g_sem.at[a, b]))
    keeps = []
    for a in range(2):
        for b in range(4):
            stays = row >= 0
            if a == 0:
                stays = stays & (row >= S)
            if b == 0:
                stays = stays & (col >= S)
            keeps.append((stays, pltpu.make_async_copy(
                g32.at[b, pl.ds(a * B, B), :], out.at[a, :, b, :], o_sem.at[a, b])))
    ltile = [pltpu.make_async_copy(lfac.at[a, :, 0, :], lt32.at[a], l_sem.at[a]) for a in range(2)]
    dload = pltpu.make_async_copy(dinv, dv, d_sem)

    @pl.when(col < S)
    def _():
        for copy in ltile:
            copy.start()
    for copy in loads:
        copy.start()
    dload.start()

    barrier = pltpu.get_barrier_semaphore()

    def greet(where):
        pl.semaphore_signal(barrier, inc=1, device_id=where, device_id_type=MESH)

    for step in range(1, 16):
        greet(at(r=(row + step) % 16))
    for c in (c_x, c_y, c_o):
        greet(at(c=c))
    greet(at(r=r_y2, c=c_y))

    def b_source(a, q):
        return yh * 8 + q * 2 + a, row % 8

    def b_other(a, q):
        sr, sc = b_source(a, q)
        return jnp.logical_not((sr == row) & (sc == col))

    for a in range(2):
        for q in range(4):
            sr, sc = b_source(a, q)

            @pl.when((col < S) & b_other(a, q))
            def _():
                greet(at(r=sr, c=sc))

    @pl.when(col < S)
    def _():
        for a in range(2):
            ltile[a].wait()
            live = mask[row + 16 * a, col] * (row + 16 * a > col).astype(jnp.int32)
            pn[col, pl.ds(a * B, B), :] = lt32[a] * live.astype(F32)

    pl.semaphore_wait(barrier, 19 + 4 - jnp.where((row == b_row) & (col < S), 1, 0))

    near = jnp.where((x == 0) | (x == 3), 0, 1)
    k_p, k_s = 2 * near + yl, 2 * (1 - near) + yl
    k_pd, k_sd = 2 * near + 1 - yl, 2 * (1 - near) + 1 - yl

    def quarter(k, ch, ssem, rsem, where):
        part = pn.at[k, pl.ds(128 * ch, 128), :]
        return remote(part, part, ssem, rsem, where)

    source, inner = x < 2, x >= 2
    always = row >= 0
    to_x, to_y, to_o = at(c=c_x), at(c=c_y), at(c=c_o)

    def out_recv(ch):
        quarter(k_p, ch, s_out.at[ch], r_out.at[ch], to_o).wait_recv()

    def x_recv(ch):
        quarter(k_s, ch, s_x.at[ch], r_x.at[ch], to_x).wait_recv()

    def y_recv(ch):
        quarter(k_pd, ch, s_y.at[ch], r_y.at[ch], to_y).wait_recv()

    def xd_recv(ch):
        quarter(k_sd, ch, s_x.at[4 + ch // 2], r_x.at[4 + ch // 2], to_x).wait_recv()

    def yd_recv(ch):
        quarter(k_sd, ch, s_y.at[4 + ch], r_y.at[4 + ch], to_y).wait_recv()

    def l_copy(u, slot, where):
        return remote(lt.at[u], lt.at[u], s_l.at[u, slot], r_l.at[u], where)

    def l_wait(u):
        l_copy(u, 0, at(r=r_core)).wait_recv()

    def l_routes(u, j):
        routes = [(always, l_copy(u, 0, at(r=r_core))), (yh == 0, l_copy(u, 1, at(r=r_y2, c=c_y)))]
        if j == 1:
            routes.append(((row == 1) | (row == 3), l_copy(u, 2, at(r=r_zp))))
            routes.append((row == 1, l_copy(u, 3, at(r=r_zm))))
        else:
            routes.append(((row == j) | (row == j + 2), l_copy(u, 2, at(r=r_zp))))
            routes.append((row == j, l_copy(u, 3, at(r=r_zm))))
        return routes

    groups = [(yh == 0) & (z < 3), (yh == 0) & (z == 3), yh == 1]

    def l_step(k, first, group=0):
        for j in (2, 3, 1):
            u = (j * (j - 1)) // 2 + k
            here = (core == CORE_OF[j]) & (k < j)

            @pl.when(here & (row == j) if first else here & (row != j) & groups[group])
            def _():
                if first:
                    lt[u] = pn[k, pl.ds(0, B), :]
                else:
                    l_wait(u)
                for cond, copy in l_routes(u, j):
                    @pl.when(cond)
                    def _():
                        copy.start()

    def p_out(ch):
        quarter(k_p, ch, s_out.at[ch], r_out.at[ch], to_o).start()

    def p_x(ch):
        quarter(k_p, ch, s_x.at[ch], r_x.at[ch], to_x).start()

    def p_y(ch):
        quarter(k_p, ch, s_y.at[ch], r_y.at[ch], to_y).start()

    def e_out(ch):
        quarter(k_pd, ch, s_out.at[3 + ch], r_out.at[3 + ch], to_o).start()

    def d_x(ch):
        quarter(k_pd, ch, s_x.at[4 + ch // 2], r_x.at[4 + ch // 2], to_x).start()

    def d_y(ch):
        quarter(k_s, ch, s_y.at[4 + ch], r_y.at[4 + ch], to_y).start()

    @pl.when(source)
    def _():
        for ch in range(3):
            p_out(ch)
            p_y(ch)
        p_x(0)
        p_x(1)
        l_step(k_p, True)

    for a in range(2):
        for b in range(4):
            loads[a * 4 + b].wait()
            cond, copy = keeps[a * 4 + b]

            @pl.when(cond)
            def _():
                copy.start()
    for b in range(4):
        for a in range(2):
            hi, lo = split(g32[b, pl.ds(a * B, B), :].T)
            gth[b, :, pl.ds(a * B, B)] = hi
            gtl[b, :, pl.ds(a * B, B)] = lo

    @pl.when(source)
    def _():
        y_recv(0)
        d_x(0)
        p_x(2)
        p_out(3)
        y_recv(1)
        e_out(1)
        p_x(3)
        x_recv(0)
        x_recv(1)
        d_y(1)
        p_y(3)
        l_step(k_pd, True)
        l_step(k_s, True)
        y_recv(2)
        d_x(2)
        e_out(2)
        xd_recv(0)
        yd_recv(1)
        l_step(k_sd, True)

    @pl.when(inner)
    def _():
        out_recv(0)
        p_x(0)
        p_y(0)
        out_recv(1)
        p_x(1)
        l_step(k_p, True)
        x_recv(0)
        d_y(0)
        out_recv(2)
        p_x(2)
        x_recv(1)
        d_y(1)
        l_step(k_s, True)
        out_recv(3)
        p_x(3)
    l_step(k_p, False)
    l_step(k_p, False, 1)

    @pl.when(source)
    def _():
        y_recv(3)
        e_out(3)
        x_recv(2)
        x_recv(3)
        d_y(3)

    @pl.when(inner)
    def _():
        x_recv(2)
        d_y(2)
        y_recv(0)
        quarter(k_pd, 1, s_out.at[4], r_out.at[4], to_o).wait_recv()
        l_step(k_pd, True)
        yd_recv(0)
        yd_recv(1)
        l_step(k_sd, True)
        x_recv(3)
        d_y(3)
    l_step(k_pd, False)
    l_step(k_s, False)

    @pl.when(source)
    def _():
        xd_recv(2)

    @pl.when(inner)
    def _():
        yd_recv(2)
        quarter(k_pd, 2, s_out.at[5], r_out.at[5], to_o).wait_recv()
        quarter(k_pd, 3, s_out.at[6], r_out.at[6], to_o).wait_recv()
    yd_recv(3)
    l_step(k_sd, False)

    zero = jnp.where(row < S, 0.0, 1.0).astype(F32)
    for k in range(S):
        for a in range(2):
            rows = pl.ds(a * B, B)
            hi, lo = split(pn[k, rows, :] * zero if a == 0 else pn[k, rows, :])
            pbh[k, rows, :] = hi
            pbl[k, rows, :] = lo
    c_core = [remote(ut.at[2 - 2 * core + u], cr.at[u], s_c.at[u], r_c.at[u], at(r=r_core)) for u in range(2)]

    def products(t):
        @pl.loop(0, S)
        def _(k):
            value = dot3((gth[t], gtl[t]), (pbh[k], pbl[k]))
            for q in range(4):
                ut[t, q, :, pl.ds(pl.multiple_of(k * B, B), B)] = value[q * 64:(q + 1) * 64]

    for u in range(2):
        products(2 - 2 * core + u)
        c_core[u].start()
    for u in range(2):
        products(2 * core + u)

    halves = [pl.ds(0, 32), pl.ds(32, 32)]
    q_op, q_rm, q_rp = (z + 2) % 4, (z + 1) % 4, (z + 3) % 4

    def unit(q, u, h):
        return ut.at[2 * core + u, q, halves[h], :]

    c_op = [remote(unit(q_op, 0, h), op.at[h], s_zo.at[0, h], r_zo.at[0, h], at(r=r_zp)) for h in range(2)]
    c_om = [remote(unit(q_op, 1, h), om.at[h], s_zo.at[1, h], r_zo.at[1, h], at(r=r_zm)) for h in range(2)]
    c_rm = [[remote(unit(q_rm, u, h), rm.at[u, h], s_zr.at[0, u, h], r_zr.at[0, u, h], at(r=r_zp)) for h in range(2)]
            for u in range(2)]
    c_rp = [[remote(unit(q_rp, u, h), rp.at[u, h], s_zr.at[1, u, h], r_zr.at[1, u, h], at(r=r_zm)) for h in range(2)]
            for u in range(2)]
    c_core[0].wait_recv()
    ut[2 * core, q_op] = ut[2 * core, q_op] + cr[0, q_op]
    for h in range(2):
        c_op[h].start()
    for q in (q_rp, q_rm, z):
        ut[2 * core, q] = ut[2 * core, q] + cr[0, q]
    c_rp[0][0].start()
    c_core[1].wait_recv()
    ut[2 * core + 1, q_op] = ut[2 * core + 1, q_op] + cr[1, q_op]
    for h in range(2):
        c_om[h].start()
    for q in (q_rm, q_rp, z):
        ut[2 * core + 1, q] = ut[2 * core + 1, q] + cr[1, q]
    c_rm[1][0].start()
    for k in (k_pd, k_s, k_sd):
        l_step(k, False, 1)
    for h in range(2):
        c_op[h].wait_recv()
        ut[2 * core, q_rm, halves[h], :] = ut[2 * core, q_rm, halves[h], :] + op[h]
        c_rm[0][h].start()
        c_om[h].wait_recv()
        ut[2 * core + 1, q_rp, halves[h], :] = ut[2 * core + 1, q_rp, halves[h], :] + om[h]
        c_rp[1][h].start()
        if h == 0:
            c_rp[0][1].start()
            c_rm[1][1].start()
    for k in (k_pd, k_p, k_sd, k_s):
        l_step(k, False, 2)

    for u, (j, k) in enumerate(LOW):
        @pl.when(core != CORE_OF[j])
        def _():
            l_wait(u)
    for u in range(6):
        hi, lo = split(lt[u])
        lbh[u] = hi
        lbl[u] = lo

    def low(j, k):
        return lbh[LOW.index((j, k))], lbl[LOW.index((j, k))]

    away = 1 - yh
    c_yh = [remote(unit(z, away, h), yr.at[h], s_yh.at[h], r_yh.at[h], at(r=r_y2)) for h in range(2)]

    def z_sum(h):
        for u in range(2):
            c_rm[u][h].wait_recv()
            c_rp[u][h].wait_recv()
        ut[2 * core + away, z, halves[h], :] = (
            ut[2 * core + away, z, halves[h], :] + (rm[away, h] + rp[away, h]))
        c_yh[h].start()

    z_sum(0)

    @pl.when(col < S)
    def _():
        for k in (3, 2, 1, 0):
            acc = jnp.concatenate([pn[k, pl.ds(0, B), :] * zero, pn[k, pl.ds(B, B), :]], axis=0)
            for j in range(k + 1, S):
                acc = acc - dot3((pbh[j], pbl[j]), low(j, k))
            hi, lo = split(acc)
            pbh[k] = hi
            pbl[k] = lo
            hi, lo = split(acc.T)
            ph[k] = hi
            plo[k] = lo

    z_sum(1)

    dload.wait()

    @pl.when((row < S) & (col < S))
    def _():
        ones = (lax.broadcasted_iota(jnp.int32, (B, B), 0) == lax.broadcasted_iota(jnp.int32, (B, B), 1))
        for m in range(S):
            for k in range(S):
                if m < k:
                    mt[m, k] = jnp.zeros((B, B), F32)
                elif m == k:
                    mt[m, k] = ones.astype(F32)
                else:
                    acc = lt[LOW.index((m, k))]
                    for j in range(k + 1, m):
                        acc = acc + dot3(low(m, j), split(mt[j, k]))
                    mt[m, k] = -acc
        zo[...] = jnp.zeros((B, B), F32)
        for m in range(S):
            part = dot3(split(dv[m]), split(mt[m, col]))
            zo[...] = zo[...] + dot3(split(mt[m, row].T), split(part))

    for h in range(2):
        c_yh[h].wait_recv()
    total = ut[2 * core + yh, z] + jnp.concatenate([rm[yh, h] + rp[yh, h] + yr[h] for h in range(2)], axis=0)
    found = {}
    for k in (3, 2, 1, 0):
        acc = total[:, k * B:(k + 1) * B]
        for j in range(k + 1, S):
            acc = acc + dot3(found[j], low(j, k))
        xt[k] = -acc
        found[k] = split(-acc)
    c_xa = [remote(xt.at[k], xa.at[t_own, q_own, :], s_xa.at[k], r_xa.at[t_own, z], at(r=k)) for k in range(S)]
    c_xb = [remote(xt.at[k], xb.at[core, q_own, :], s_xb.at[k], r_xb.at[core, z], at(r=b_row, c=k)) for k in range(S)]

    def b_self(k):
        return (row == b_row) & (col == k)

    for k in (3, 2, 1, 0):
        @pl.when(jnp.logical_not(b_self(k)))
        def _():
            c_xb[k].start()

        @pl.when(b_self(k))
        def _():
            xb[core, q_own, :] = xt[k]
    for k in range(S):
        @pl.when(row != k)
        def _():
            c_xa[k].start()

        @pl.when(row == k)
        def _():
            xa[t_own, q_own, :] = xt[k]

    c_zc = remote(zp.at[1 - core], zc, s_zc, r_zc, at(r=r_core))
    c_zd = [remote(zp.at[core, :, pl.ds(((quad + d) % 8) * 32, 32), :], zr.at[d - 1], s_zd.at[d - 1], r_zd.at[d - 1],
                   at(r=((quad + d) % 8) * 2 + core)) for d in range(1, 8)]
    c_zf = [remote(zs.at[m], zf.at[pl.ds(quad * 32, 32), :], s_zf.at[m], r_zf.at[quad], at(r=2 * m + core))
            for m in range(2)]

    @pl.when(col < S)
    def _():
        for a in range(2):
            for q in range(4):
                @pl.when(b_other(a, q))
                def _():
                    remote(xt.at[0], xb.at[a, pl.ds(64 * q, 64), :], s_xb.at[0], r_xb.at[a, q], at(r=b_row)).wait_recv()
            hi, lo = split(xb[a])
            xh[pl.ds(a * B, B), :] = hi
            xl[pl.ds(a * B, B), :] = lo
        for l in range(S):
            zp[l % 2, l // 2] = dot3((ph[l], plo[l]), (xh[...], xl[...]))
        c_zc.start()
        c_zc.wait_recv()
        zp[core] = zp[core] + zc[...]
        for copy in c_zd:
            copy.start()
        acc = zp[core, :, pl.ds(quad * 32, 32), :]
        for d in range(7):
            c_zd[d].wait_recv()
            acc = acc + zr[d]
        zs[...] = acc
        for m in range(2):
            @pl.when(quad != m)
            def _():
                c_zf[m].start()

            @pl.when(quad == m)
            def _():
                zf[pl.ds(quad * 32, 32), :] = zs[m]

        @pl.when(row < S)
        def _():
            for q in range(8):
                @pl.when(quad != q)
                def _():
                    remote(zs.at[0], zf.at[pl.ds(q * 32, 32), :], s_zf.at[0], r_zf.at[q], at(r=r_core)).wait_recv()
            zo[...] = zo[...] - zf[...]

    w_row = [pltpu.make_async_copy(xat.at[t], out.at[0, :, t, :], w_sem.at[t]) for t in range(4)]
    w_col = [pltpu.make_async_copy(xb.at[a], out.at[a, :, 0, :], w_sem.at[4 + a]) for a in range(2)]
    w_dia = pltpu.make_async_copy(zo, out.at[0, :, 0, :], w_sem.at[6])
    writes = [((row < S) & (col >= S), w_row[0])] + [(row < S, w_row[t]) for t in range(1, 4)]
    writes += [((col < S) & (row >= S), w_col[0]), (col < S, w_col[1]), ((row < S) & (col < S), w_dia)]

    @pl.when(row < S)
    def _():
        for t in range(4):
            for q in range(4):
                @pl.when(row != (t % 2) * 8 + q * 2 + t // 2)
                def _():
                    remote(xt.at[0], xa.at[t, pl.ds(64 * q, 64), :], s_xa.at[0], r_xa.at[t, q], at(r=r_core)).wait_recv()
            xat[t] = xa[t].T
    for cond, copy in writes:
        @pl.when(cond)
        def _():
            copy.start()

    @pl.when(source)
    def _():
        for ch in range(4):
            quarter(k_p, ch, s_out.at[ch], r_out.at[ch], to_o).wait_send()
        for ch in (1, 2, 3):
            quarter(k_pd, ch, s_out.at[3 + ch], r_out.at[3 + ch], to_o).wait_send()
            quarter(k_p, ch, s_y.at[ch], r_y.at[ch], to_y).wait_send()
        for ch in (0, 2):
            quarter(k_pd, ch, s_x.at[4 + ch // 2], r_x.at[4 + ch // 2], to_x).wait_send()

    @pl.when(inner)
    def _():
        for ch in (0, 2):
            quarter(k_s, ch, s_y.at[4 + ch], r_y.at[4 + ch], to_y).wait_send()
    for ch in range(4):
        quarter(k_p, ch, s_x.at[ch], r_x.at[ch], to_x).wait_send()
    quarter(k_p, 0, s_y.at[0], r_y.at[0], to_y).wait_send()
    for ch in (1, 3):
        quarter(k_s, ch, s_y.at[4 + ch], r_y.at[4 + ch], to_y).wait_send()
    for j, k in LOW:
        @pl.when(core == CORE_OF[j])
        def _():
            for cond, copy in l_routes(LOW.index((j, k)), j):
                @pl.when(cond)
                def _():
                    copy.wait_send()
    for copy in c_core + c_op + c_om + c_rm[0] + c_rm[1] + c_rp[0] + c_rp[1] + c_yh:
        copy.wait_send()

    for k in range(S):
        @pl.when(jnp.logical_not(b_self(k)))
        def _():
            c_xb[k].wait_send()

        @pl.when(row != k)
        def _():
            c_xa[k].wait_send()

    @pl.when(col < S)
    def _():
        c_zc.wait_send()
        for copy in c_zd:
            copy.wait_send()
        for m in range(2):
            @pl.when(quad != m)
            def _():
                c_zf[m].wait_send()
    for cond, copy in writes + keeps:
        @pl.when(cond)
        def _():
            copy.wait()


def body(prior, lfac, tile_mask, dinv):
    def vmem(*shape, kind=F32):
        return pltpu.VMEM(shape, kind)

    dma = pltpu.SemaphoreType.DMA
    wide = S * B
    scratch = [
        vmem(4, 2 * B, B), vmem(4, B, 2 * B, kind=BF16), vmem(4, B, 2 * B, kind=BF16),
        vmem(2, B, B), vmem(4, 2 * B, B), vmem(4, 2 * B, B, kind=BF16), vmem(4, 2 * B, B, kind=BF16),
        vmem(4, B, 2 * B, kind=BF16), vmem(4, B, 2 * B, kind=BF16),
        vmem(6, B, B), vmem(6, B, B, kind=BF16), vmem(6, B, B, kind=BF16),
        vmem(4, 4, 64, wide), vmem(2, 4, 64, wide),
        vmem(2, 32, wide), vmem(2, 32, wide), vmem(2, 2, 32, wide), vmem(2, 2, 32, wide), vmem(2, 32, wide),
        vmem(4, 64, B), vmem(4, B, B), vmem(2, B, B), vmem(4, B, B),
        vmem(2 * B, B, kind=BF16), vmem(2 * B, B, kind=BF16),
        vmem(2, 2, B, B), vmem(2, B, B), vmem(7, 2, 32, B), vmem(2, 32, B), vmem(B, B),
        vmem(4, 4, B, B), vmem(4, B, B), vmem(B, B),
        dma((2, 4)), dma((2,)), dma, dma((2, 4)), dma((7,)),
        dma((7,)), dma((7,)), dma((6,)), dma((6,)), dma((8,)), dma((8,)),
        dma((6, 4)), dma((6,)), dma((2,)), dma((2,)),
        dma((2, 2)), dma((2, 2)), dma((2, 2, 2)), dma((2, 2, 2)), dma((2,)), dma((2,)),
        dma((4,)), dma((4, 4)), dma((4,)), dma((2, 4)),
        dma, dma, dma((7,)), dma((7,)), dma((2,)), dma((8,)),
    ]
    return pl.pallas_call(
        kernel,
        out_shape=jax.ShapeDtypeStruct(prior.shape, F32),
        in_specs=[pl.BlockSpec(memory_space=pl.ANY), pl.BlockSpec(memory_space=pl.ANY),
                  pl.BlockSpec(memory_space=pltpu.SMEM), pl.BlockSpec(memory_space=pl.ANY)],
        out_specs=pl.BlockSpec(memory_space=pl.ANY),
        scratch_shapes=scratch,
        compiler_params=pltpu.CompilerParams(
            collective_id=0, has_side_effects=True, vmem_limit_bytes=56 * 1024 * 1024),
    )(prior, lfac, tile_mask, dinv)


def solution(mesh):
    placed = (P("prow", None, "pcol", None), P("prow", None, "pcol", None), P(), P())
    return jax.shard_map(
        body, mesh=mesh, in_specs=placed, out_specs=P("prow", None, "pcol", None), check_vma=False
    )
```

time: 126 us -> 101 us (0.80)
  Pallas kernels: 122 us -> 97.5 us
    pallas_call x1, Pallas kernels: 122 us -> 97.5 us  [body(): pl.pallas_call(kernel, out_shape=jax.ShapeDtypeStruct(prior.shape, F32),...]
where the time goes in v3:
time: 101 us
  Pallas kernels  97.5 us (97%)
  local copies, waits for them, and re-layouts  3.27 us (3%)
    pallas_call x1, Pallas kernels, body(): pl.pallas_call(kernel, out_shape=jax.ShapeDtypeStruct(prior.shape, F32),...  97.5 us
    unnamed x1, local copies, waits for them, and re-layouts  3.27 us

profile of v3, /device:TPU:3, one launch (start us, length us, event | category | flops | bytes accessed | tf_op | source)
XLA Modules:
  0.0 100.8 jit_solution(1307005339106125119)
XLA Ops:
  0.0 97.5 %shard_map.46 = f32[2,256,4,256]{3,2,1,0:T(4,128)} custom-call(f32[2,256,4,256]{3,2,1,0:T(4,128)} %prior.1, f32[2,256,4,256]{3,2,1,0:T(4,128)} %lfac.1, s32[32,32]{1,0:T(8,128)} %mask.1, f32[4,256,256]{2,1,0:T(8,128)} %dinv.1), custom_call_target="tpu_custom_call" | custom-call | tf_op jit(solution)/shard_map/pallas_call | solution.py:598
  97.5 3.3 %copy.6 = f32[2,256,4,256]{3,2,1,0:T(4,128)} copy(f32[2,256,4,256]{3,2,1,0:T(4,128)} %shard_map.46) | data formatting | bytes 4194304

commit v4 on v3

--- a/solution.py
+++ b/solution.py
@@ -27,9 +27,9 @@
     return one(a[0], b[0]) + (one(a[0], b[1]) + one(a[1], b[0]))
 
 
-def kernel(prior, lfac, mask, dinv, out,
+def kernel(prior, lfac, tile_mask, dinv, out,
            g32, gth, gtl, lt32, pn, pbh, pbl, ph, plo, lt, lbh, lbl, ut, cr, op, om, rm, rp, yr, xt, xa, xb, xat, xh, xl,
-           zp, zc, zr, zs, zf, mt, dv, zo,
+           zp, zc, zr, zs, zf, mt, dv, zo, mask, m_sem,
            g_sem, l_sem, d_sem, o_sem, w_sem,
            s_out, r_out, s_x, r_x, s_y, r_y,
            s_l, r_l, s_c, r_c, s_zo, r_zo, s_zr, r_zr, s_yh, r_yh,
@@ -73,10 +73,12 @@
             keeps.append((stays, pltpu.make_async_copy(
                 g32.at[b, pl.ds(a * B, B), :], out.at[a, :, b, :], o_sem.at[a, b])))
     ltile = [pltpu.make_async_copy(lfac.at[a, :, 0, :], lt32.at[a], l_sem.at[a]) for a in range(2)]
+    mload = pltpu.make_async_copy(tile_mask, mask, m_sem)
     dload = pltpu.make_async_copy(dinv, dv, d_sem)
 
     @pl.when(col < S)
     def _():
+        mload.start()
         for copy in ltile:
             copy.start()
     for copy in loads:
@@ -111,6 +113,7 @@
 
     @pl.when(col < S)
     def _():
+        mload.wait()
         for a in range(2):
             ltile[a].wait()
             live = mask[row + 16 * a, col] * (row + 16 * a > col).astype(jnp.int32)
@@ -220,8 +223,30 @@
             gth[b, :, pl.ds(a * B, B)] = hi
             gtl[b, :, pl.ds(a * B, B)] = lo
 
+    zero = jnp.where(row < S, 0.0, 1.0).astype(F32)
+
+    def core_copy(k):
+        lanes = pl.ds(pl.multiple_of(k * B, B), B)
+        return remote(ut.at[pl.ds(2 - 2 * core, 2), :, :, lanes], cr.at[:, :, :, lanes], s_c.at[k], r_c.at[k], at(r=r_core))
+
+    def products(k):
+        for a in range(2):
+            rows = pl.ds(a * B, B)
+            hi, lo = split(pn[k, rows, :] * zero if a == 0 else pn[k, rows, :])
+            pbh[k, rows, :] = hi
+            pbl[k, rows, :] = lo
+
+        @pl.loop(0, 4)
+        def _(step):
+            t = lax.rem(2 - 2 * core + step, 4)
+            value = dot3((gth[t], gtl[t]), (pbh[k], pbl[k]))
+            for q in range(4):
+                ut[t, q, :, pl.ds(pl.multiple_of(k * B, B), B)] = value[q * 64:(q + 1) * 64]
+        core_copy(k).start()
+
     @pl.when(source)
     def _():
+        products(k_p)
         y_recv(0)
         d_x(0)
         p_x(2)
@@ -259,6 +284,7 @@
         l_step(k_s, True)
         out_recv(3)
         p_x(3)
+        products(k_p)
     l_step(k_p, False)
     l_step(k_p, False, 1)
 
@@ -284,6 +310,14 @@
         d_y(3)
     l_step(k_pd, False)
     l_step(k_s, False)
+    products(k_s)
+
+    @pl.when(inner)
+    def _():
+        for ch in (2, 3):
+            quarter(k_pd, ch, s_out.at[3 + ch], r_out.at[3 + ch], to_o).wait_recv()
+    products(k_pd)
+    l_step(k_sd, False)
 
     @pl.when(source)
     def _():
@@ -292,32 +326,8 @@
     @pl.when(inner)
     def _():
         yd_recv(2)
-        quarter(k_pd, 2, s_out.at[5], r_out.at[5], to_o).wait_recv()
-        quarter(k_pd, 3, s_out.at[6], r_out.at[6], to_o).wait_recv()
     yd_recv(3)
-    l_step(k_sd, False)
-
-    zero = jnp.where(row < S, 0.0, 1.0).astype(F32)
-    for k in range(S):
-        for a in range(2):
-            rows = pl.ds(a * B, B)
-            hi, lo = split(pn[k, rows, :] * zero if a == 0 else pn[k, rows, :])
-            pbh[k, rows, :] = hi
-            pbl[k, rows, :] = lo
-    c_core = [remote(ut.at[2 - 2 * core + u], cr.at[u], s_c.at[u], r_c.at[u], at(r=r_core)) for u in range(2)]
-
-    def products(t):
-        @pl.loop(0, S)
-        def _(k):
-            value = dot3((gth[t], gtl[t]), (pbh[k], pbl[k]))
-            for q in range(4):
-                ut[t, q, :, pl.ds(pl.multiple_of(k * B, B), B)] = value[q * 64:(q + 1) * 64]
-
-    for u in range(2):
-        products(2 - 2 * core + u)
-        c_core[u].start()
-    for u in range(2):
-        products(2 * core + u)
+    products(k_sd)
 
     halves = [pl.ds(0, 32), pl.ds(32, 32)]
     q_op, q_rm, q_rp = (z + 2) % 4, (z + 1) % 4, (z + 3) % 4
@@ -331,14 +341,14 @@
             for u in range(2)]
     c_rp = [[remote(unit(q_rp, u, h), rp.at[u, h], s_zr.at[1, u, h], r_zr.at[1, u, h], at(r=r_zm)) for h in range(2)]
             for u in range(2)]
-    c_core[0].wait_recv()
+    for k in range(S):
+        core_copy(k).wait_recv()
     ut[2 * core, q_op] = ut[2 * core, q_op] + cr[0, q_op]
     for h in range(2):
         c_op[h].start()
     for q in (q_rp, q_rm, z):
         ut[2 * core, q] = ut[2 * core, q] + cr[0, q]
     c_rp[0][0].start()
-    c_core[1].wait_recv()
     ut[2 * core + 1, q_op] = ut[2 * core + 1, q_op] + cr[1, q_op]
     for h in range(2):
         c_om[h].start()
@@ -460,6 +470,18 @@
     c_zf = [remote(zs.at[m], zf.at[pl.ds(quad * 32, 32), :], s_zf.at[m], r_zf.at[quad], at(r=2 * m + core))
             for m in range(2)]
 
+    w_row = [pltpu.make_async_copy(xat.at[t], out.at[0, :, t, :], w_sem.at[t]) for t in range(4)]
+    w_col = [pltpu.make_async_copy(xb.at[a], out.at[a, :, 0, :], w_sem.at[4 + a]) for a in range(2)]
+    w_dia = pltpu.make_async_copy(zo, out.at[0, :, 0, :], w_sem.at[6])
+    rows_new = [((row < S) & (col >= S), w_row[0])] + [(row < S, w_row[t]) for t in range(1, 4)]
+    cols_new = [((col < S) & (row >= S), w_col[0]), (col < S, w_col[1])]
+    writes = rows_new + cols_new + [((row < S) & (col < S), w_dia)]
+
+    def diagonal(side):
+        @pl.loop(0, 2)
+        def _(m):
+            zp[side, m] = dot3((ph[2 * m + side], plo[2 * m + side]), (xh[...], xl[...]))
+
     @pl.when(col < S)
     def _():
         for a in range(2):
@@ -470,9 +492,13 @@
             hi, lo = split(xb[a])
             xh[pl.ds(a * B, B), :] = hi
             xl[pl.ds(a * B, B), :] = lo
-        for l in range(S):
-            zp[l % 2, l // 2] = dot3((ph[l], plo[l]), (xh[...], xl[...]))
+        diagonal(1 - core)
         c_zc.start()
+        diagonal(core)
+        for cond, copy in cols_new:
+            @pl.when(cond)
+            def _():
+                copy.start()
         c_zc.wait_recv()
         zp[core] = zp[core] + zc[...]
         for copy in c_zd:
@@ -491,20 +517,6 @@
             def _():
                 zf[pl.ds(quad * 32, 32), :] = zs[m]
 
-        @pl.when(row < S)
-        def _():
-            for q in range(8):
-                @pl.when(quad != q)
-                def _():
-                    remote(zs.at[0], zf.at[pl.ds(q * 32, 32), :], s_zf.at[0], r_zf.at[q], at(r=r_core)).wait_recv()
-            zo[...] = zo[...] - zf[...]
-
-    w_row = [pltpu.make_async_copy(xat.at[t], out.at[0, :, t, :], w_sem.at[t]) for t in range(4)]
-    w_col = [pltpu.make_async_copy(xb.at[a], out.at[a, :, 0, :], w_sem.at[4 + a]) for a in range(2)]
-    w_dia = pltpu.make_async_copy(zo, out.at[0, :, 0, :], w_sem.at[6])
-    writes = [((row < S) & (col >= S), w_row[0])] + [(row < S, w_row[t]) for t in range(1, 4)]
-    writes += [((col < S) & (row >= S), w_col[0]), (col < S, w_col[1]), ((row < S) & (col < S), w_dia)]
-
     @pl.when(row < S)
     def _():
         for t in range(4):
@@ -513,10 +525,19 @@
                 def _():
                     remote(xt.at[0], xa.at[t, pl.ds(64 * q, 64), :], s_xa.at[0], r_xa.at[t, q], at(r=r_core)).wait_recv()
             xat[t] = xa[t].T
-    for cond, copy in writes:
-        @pl.when(cond)
-        def _():
-            copy.start()
+        for cond, copy in rows_new:
+            @pl.when(cond)
+            def _():
+                copy.start()
+
+    @pl.when((row < S) & (col < S))
+    def _():
+        for q in range(8):
+            @pl.when(quad != q)
+            def _():
+                remote(zs.at[0], zf.at[pl.ds(q * 32, 32), :], s_zf.at[0], r_zf.at[q], at(r=r_core)).wait_recv()
+        zo[...] = zo[...] - zf[...]
+        w_dia.start()
 
     @pl.when(source)
     def _():
@@ -544,7 +565,7 @@
                 @pl.when(cond)
                 def _():
                     copy.wait_send()
-    for copy in c_core + c_op + c_om + c_rm[0] + c_rm[1] + c_rp[0] + c_rp[1] + c_yh:
+    for copy in [core_copy(k) for k in range(S)] + c_op + c_om + c_rm[0] + c_rm[1] + c_rp[0] + c_rp[1] + c_yh:
         copy.wait_send()
 
     for k in range(S):
@@ -587,10 +608,10 @@
         vmem(4, 64, B), vmem(4, B, B), vmem(2, B, B), vmem(4, B, B),
         vmem(2 * B, B, kind=BF16), vmem(2 * B, B, kind=BF16),
         vmem(2, 2, B, B), vmem(2, B, B), vmem(7, 2, 32, B), vmem(2, 32, B), vmem(B, B),
-        vmem(4, 4, B, B), vmem(4, B, B), vmem(B, B),
+        vmem(4, 4, B, B), vmem(4, B, B), vmem(B, B), pltpu.SMEM((32, 32), jnp.int32), dma,
         dma((2, 4)), dma((2,)), dma, dma((2, 4)), dma((7,)),
         dma((7,)), dma((7,)), dma((6,)), dma((6,)), dma((8,)), dma((8,)),
-        dma((6, 4)), dma((6,)), dma((2,)), dma((2,)),
+        dma((6, 4)), dma((6,)), dma((4,)), dma((4,)),
         dma((2, 2)), dma((2, 2)), dma((2, 2, 2)), dma((2, 2, 2)), dma((2,)), dma((2,)),
         dma((4,)), dma((4, 4)), dma((4,)), dma((2, 4)),
         dma, dma, dma((7,)), dma((7,)), dma((2,)), dma((8,)),
@@ -599,7 +620,7 @@
         kernel,
         out_shape=jax.ShapeDtypeStruct(prior.shape, F32),
         in_specs=[pl.BlockSpec(memory_space=pl.ANY), pl.BlockSpec(memory_space=pl.ANY),
-                  pl.BlockSpec(memory_space=pltpu.SMEM), pl.BlockSpec(memory_space=pl.ANY)],
+                  pl.BlockSpec(memory_space=pl.ANY), pl.BlockSpec(memory_space=pl.ANY)],
         out_specs=pl.BlockSpec(memory_space=pl.ANY),
         scratch_shapes=scratch,
         compiler_params=pltpu.CompilerParams(

time: 101 us -> 94.6 us (0.937)
  the two profiles are of different devices: /device:TPU:3 before, /device:TPU:32 now
where the time goes in v4:
time: 94.6 us; the launch traced here: 92.9 us
  Pallas kernels  89.6 us (95%)
  local copies, waits for them, and re-layouts  3.27 us (3%)
    pallas_call x1, Pallas kernels, body(): pl.pallas_call(kernel, out_shape=jax.ShapeDtypeStruct(prior.shape, F32),...  89.6 us
    unnamed x1, local copies, waits for them, and re-layouts  3.27 us

profile of v4, /device:TPU:32, one launch (start us, length us, event | category | flops | bytes accessed | tf_op | source)
XLA Modules:
  0.0 92.9 jit_solution(14570985942612898223)
XLA Ops:
  0.0 89.6 %shard_map.46 = f32[2,256,4,256]{3,2,1,0:T(4,128)} custom-call(f32[2,256,4,256]{3,2,1,0:T(4,128)} %prior.1, f32[2,256,4,256]{3,2,1,0:T(4,128)} %lfac.1, s32[32,32]{1,0:T(8,128)} %tile_mask.1, f32[4,256,256]{2,1,0:T(8,128)} %dinv.1), custom_call_target="tpu_custom_call" | custom-call | tf_op jit(solution)/shard_map/pallas_call | solution.py:619
  89.6 3.3 %copy.6 = f32[2,256,4,256]{3,2,1,0:T(4,128)} copy(f32[2,256,4,256]{3,2,1,0:T(4,128)} %shard_map.46) | data formatting | bytes 4194304

commit v5 on v4

--- a/solution.py
+++ b/solution.py
@@ -28,11 +28,12 @@
 
 
 def kernel(prior, lfac, tile_mask, dinv, out,
-           g32, gth, gtl, lt32, pn, pbh, pbl, ph, plo, lt, lbh, lbl, ut, cr, op, om, rm, rp, yr, xt, xa, xb, xat, xh, xl,
+           g32, gth, gtl, lt32, pn, pbh, pbl, ph, plo, lt, lbh, lbl, ut, cr, op, om, rm, rp, yr,
+           yq, op1, om1, rm1, rp1, sums, xt, xa, xb, xat, xh, xl,
            zp, zc, zr, zs, zf, mt, dv, zo, mask, m_sem,
            g_sem, l_sem, d_sem, o_sem, w_sem,
            s_out, r_out, s_x, r_x, s_y, r_y,
-           s_l, r_l, s_c, r_c, s_zo, r_zo, s_zr, r_zr, s_yh, r_yh,
+           s_l, r_l, s_c, r_c, s_zo, r_zo, s_zr, r_zr, s_yh, r_yh, s_yq, r_yq, s_eo, r_eo, s_er, r_er,
            s_xa, r_xa, s_xb, r_xb, s_zc, r_zc, s_zd, r_zd, s_zf, r_zf):
     row = lax.axis_index("prow")
     col = lax.axis_index("pcol")
@@ -154,26 +155,23 @@
     def l_wait(u):
         l_copy(u, 0, at(r=r_core)).wait_recv()
 
+    place = row % 8
+
     def l_routes(u, j):
-        routes = [(always, l_copy(u, 0, at(r=r_core))), (yh == 0, l_copy(u, 1, at(r=r_y2, c=c_y)))]
-        if j == 1:
-            routes.append(((row == 1) | (row == 3), l_copy(u, 2, at(r=r_zp))))
-            routes.append((row == 1, l_copy(u, 3, at(r=r_zm))))
-        else:
-            routes.append(((row == j) | (row == j + 2), l_copy(u, 2, at(r=r_zp))))
-            routes.append((row == j, l_copy(u, 3, at(r=r_zm))))
-        return routes
-
-    groups = [(yh == 0) & (z < 3), (yh == 0) & (z == 3), yh == 1]
-
-    def l_step(k, first, group=0):
-        for j in (2, 3, 1):
+        ahead, behind = {1: ((1, 3), (1,)), 2: ((2,), (2, 0)), 3: ((3, 5), (3,))}[j]
+        plus = (place == ahead[0]) | (place == ahead[-1])
+        minus = (place == behind[0]) | (place == behind[-1])
+        return [(always, l_copy(u, 0, at(r=r_core))), (row == j, l_copy(u, 1, at(r=r_y2, c=c_y))),
+                (plus, l_copy(u, 2, at(r=r_zp))), (minus, l_copy(u, 3, at(r=r_zm)))]
+
+    def l_step(k, mine, rows=(2, 3, 1)):
+        for j in rows:
             u = (j * (j - 1)) // 2 + k
             here = (core == CORE_OF[j]) & (k < j)
 
-            @pl.when(here & (row == j) if first else here & (row != j) & groups[group])
-            def _():
-                if first:
+            @pl.when(here & (row == j) if mine is None else here & (row != j) & mine)
+            def _():
+                if mine is None:
                     lt[u] = pn[k, pl.ds(0, B), :]
                 else:
                     l_wait(u)
@@ -182,6 +180,9 @@
                     def _():
                         copy.start()
 
+    l_order = [jnp.where(yh == 0, a, b) for a, b in ((k_p, k_pd), (k_pd, k_p), (k_s, k_sd), (k_sd, k_s))]
+    early, later, last = z == 1, (z == 0) | (z == 2), z == 3
+
     def p_out(ch):
         quarter(k_p, ch, s_out.at[ch], r_out.at[ch], to_o).start()
 
@@ -207,7 +208,7 @@
             p_y(ch)
         p_x(0)
         p_x(1)
-        l_step(k_p, True)
+        l_step(k_p, None)
 
     for a in range(2):
         for b in range(4):
@@ -258,14 +259,14 @@
         x_recv(1)
         d_y(1)
         p_y(3)
-        l_step(k_pd, True)
-        l_step(k_s, True)
+        l_step(k_pd, None)
+        l_step(k_s, None)
         y_recv(2)
         d_x(2)
         e_out(2)
         xd_recv(0)
         yd_recv(1)
-        l_step(k_sd, True)
+        l_step(k_sd, None)
 
     @pl.when(inner)
     def _():
@@ -274,19 +275,18 @@
         p_y(0)
         out_recv(1)
         p_x(1)
-        l_step(k_p, True)
+        l_step(k_p, None)
         x_recv(0)
         d_y(0)
         out_recv(2)
         p_x(2)
         x_recv(1)
         d_y(1)
-        l_step(k_s, True)
+        l_step(k_s, None)
         out_recv(3)
         p_x(3)
         products(k_p)
-    l_step(k_p, False)
-    l_step(k_p, False, 1)
+    l_step(l_order[0], early, (2, 3))
 
     @pl.when(source)
     def _():
@@ -302,14 +302,15 @@
         d_y(2)
         y_recv(0)
         quarter(k_pd, 1, s_out.at[4], r_out.at[4], to_o).wait_recv()
-        l_step(k_pd, True)
+        l_step(k_pd, None)
         yd_recv(0)
         yd_recv(1)
-        l_step(k_sd, True)
+        l_step(k_sd, None)
         x_recv(3)
         d_y(3)
-    l_step(k_pd, False)
-    l_step(k_s, False)
+    l_step(l_order[1], early, (2, 3))
+    l_step(l_order[2], early, (2, 3))
+    l_step(l_order[0], later, (2, 3))
     products(k_s)
 
     @pl.when(inner)
@@ -317,7 +318,9 @@
         for ch in (2, 3):
             quarter(k_pd, ch, s_out.at[3 + ch], r_out.at[3 + ch], to_o).wait_recv()
     products(k_pd)
-    l_step(k_sd, False)
+    l_step(l_order[3], early, (2, 3))
+    l_step(l_order[1], later, (2, 3))
+    l_step(0, row == 9, (1,))
 
     @pl.when(source)
     def _():
@@ -329,140 +332,162 @@
     yd_recv(3)
     products(k_sd)
 
-    halves = [pl.ds(0, 32), pl.ds(32, 32)]
+    top, end = pl.ds(0, 32), pl.ds(32, 32)
+    low16, high16 = pl.ds(32, 16), pl.ds(48, 16)
     q_op, q_rm, q_rp = (z + 2) % 4, (z + 1) % 4, (z + 3) % 4
-
-    def unit(q, u, h):
-        return ut.at[2 * core + u, q, halves[h], :]
-
-    c_op = [remote(unit(q_op, 0, h), op.at[h], s_zo.at[0, h], r_zo.at[0, h], at(r=r_zp)) for h in range(2)]
-    c_om = [remote(unit(q_op, 1, h), om.at[h], s_zo.at[1, h], r_zo.at[1, h], at(r=r_zm)) for h in range(2)]
-    c_rm = [[remote(unit(q_rm, u, h), rm.at[u, h], s_zr.at[0, u, h], r_zr.at[0, u, h], at(r=r_zp)) for h in range(2)]
-            for u in range(2)]
-    c_rp = [[remote(unit(q_rp, u, h), rp.at[u, h], s_zr.at[1, u, h], r_zr.at[1, u, h], at(r=r_zm)) for h in range(2)]
-            for u in range(2)]
+    away = 1 - yh
+    t_away = 2 * core + away
+
+    def unit(q, u):
+        return ut.at[2 * core + u, q, top, :]
+
+    c_op = remote(unit(q_op, 0), op, s_zo.at[0], r_zo.at[0], at(r=r_zp))
+    c_om = remote(unit(q_op, 1), om, s_zo.at[1], r_zo.at[1], at(r=r_zm))
+    c_rm = [remote(unit(q_rm, u), rm.at[u], s_zr.at[0, u], r_zr.at[0, u], at(r=r_zp)) for u in range(2)]
+    c_rp = [remote(unit(q_rp, u), rp.at[u], s_zr.at[1, u], r_zr.at[1, u], at(r=r_zm)) for u in range(2)]
+    c_yh = remote(unit(z, away), yr, s_yh, r_yh, at(r=r_y2))
+
+    def y_copy(q):
+        return remote(ut.at[t_away, q, end, :], yq.at[q], s_yq.at[q], r_yq.at[q], at(r=r_y2))
+
+    def y_add(q):
+        y_copy(q).wait_recv()
+        ut[t_own, q, end, :] = ut[t_own, q, end, :] + yq[q]
+
+    e_op = remote(ut.at[t_own, q_op, low16, :], op1, s_eo.at[0], r_eo.at[0], at(r=r_zp))
+    e_om = remote(ut.at[t_own, q_op, high16, :], om1, s_eo.at[1], r_eo.at[1], at(r=r_zm))
+    e_rm = [remote(ut.at[t_own, q_rm, part, :], rm1.at[n], s_er.at[0, n], r_er.at[0, n], at(r=r_zp))
+            for n, part in enumerate((low16, high16))]
+    e_rp = [remote(ut.at[t_own, q_rp, part, :], rp1.at[n], s_er.at[1, n], r_er.at[1, n], at(r=r_zm))
+            for n, part in enumerate((low16, high16))]
+
+    def core_add(q):
+        for u in range(2):
+            ut[2 * core + u, q] = ut[2 * core + u, q] + cr[u, q]
+
     for k in range(S):
         core_copy(k).wait_recv()
-    ut[2 * core, q_op] = ut[2 * core, q_op] + cr[0, q_op]
-    for h in range(2):
-        c_op[h].start()
-    for q in (q_rp, q_rm, z):
-        ut[2 * core, q] = ut[2 * core, q] + cr[0, q]
-    c_rp[0][0].start()
-    ut[2 * core + 1, q_op] = ut[2 * core + 1, q_op] + cr[1, q_op]
-    for h in range(2):
-        c_om[h].start()
-    for q in (q_rm, q_rp, z):
-        ut[2 * core + 1, q] = ut[2 * core + 1, q] + cr[1, q]
-    c_rm[1][0].start()
-    for k in (k_pd, k_s, k_sd):
-        l_step(k, False, 1)
-    for h in range(2):
-        c_op[h].wait_recv()
-        ut[2 * core, q_rm, halves[h], :] = ut[2 * core, q_rm, halves[h], :] + op[h]
-        c_rm[0][h].start()
-        c_om[h].wait_recv()
-        ut[2 * core + 1, q_rp, halves[h], :] = ut[2 * core + 1, q_rp, halves[h], :] + om[h]
-        c_rp[1][h].start()
-        if h == 0:
-            c_rp[0][1].start()
-            c_rm[1][1].start()
-    for k in (k_pd, k_p, k_sd, k_s):
-        l_step(k, False, 2)
+    core_add(q_op)
+    c_op.start()
+    c_om.start()
+    y_copy(q_op).start()
+    core_add(q_rm)
+    c_rm[1].start()
+    y_copy(q_rm).start()
+    core_add(q_rp)
+    c_rp[0].start()
+    y_copy(q_rp).start()
+    core_add(z)
+    y_copy(z).start()
+    l_step(l_order[2], later, (2, 3))
+    c_op.wait_recv()
+    ut[2 * core, q_rm, top, :] = ut[2 * core, q_rm, top, :] + op[...]
+    c_rm[0].start()
+    c_om.wait_recv()
+    ut[2 * core + 1, q_rp, top, :] = ut[2 * core + 1, q_rp, top, :] + om[...]
+    c_rp[1].start()
+    y_add(q_op)
+    e_op.start()
+    e_om.start()
+    y_add(q_rm)
+    e_rm[1].start()
+    y_add(q_rp)
+    e_rp[0].start()
+    l_step(l_order[3], later, (2, 3))
+    l_step(0, place == 3, (1,))
+    e_op.wait_recv()
+    ut[t_own, q_rm, low16, :] = ut[t_own, q_rm, low16, :] + op1[...]
+    e_rm[0].start()
+    e_om.wait_recv()
+    ut[t_own, q_rp, high16, :] = ut[t_own, q_rp, high16, :] + om1[...]
+    e_rp[1].start()
+    for u in range(2):
+        c_rm[u].wait_recv()
+        c_rp[u].wait_recv()
+    ut[t_away, z, top, :] = ut[t_away, z, top, :] + (rm[away] + rp[away])
+    c_yh.start()
+    for n in range(4):
+        l_step(l_order[n], last, (2, 3))
+    l_step(0, (row != 9) & (place != 3), (1,))
+
+    y_add(z)
+    for n in range(2):
+        e_rm[n].wait_recv()
+        e_rp[n].wait_recv()
+    sums[pl.ds(32, 32), :] = ut[t_own, z, end, :] + jnp.concatenate([rm1[n] + rp1[n] for n in range(2)], axis=0)
+    c_yh.wait_recv()
+    sums[pl.ds(0, 32), :] = ut[t_own, z, top, :] + (rm[yh] + rp[yh] + yr[...])
 
     for u, (j, k) in enumerate(LOW):
         @pl.when(core != CORE_OF[j])
         def _():
             l_wait(u)
-    for u in range(6):
-        hi, lo = split(lt[u])
+
+    def low(j, k):
+        return lbh[LOW.index((j, k))], lbl[LOW.index((j, k))]
+
+    for m, k in [(1, 0), (2, 1), (3, 2), (2, 0), (3, 1), (3, 0)]:
+        u = LOW.index((m, k))
+        acc = lt[u]
+        for j in range(k + 1, m):
+            acc = acc + dot3(split(lt[LOW.index((m, j))]), low(j, k))
+        mt[m, k] = -acc
+        hi, lo = split(-acc)
         lbh[u] = hi
         lbl[u] = lo
 
-    def low(j, k):
-        return lbh[LOW.index((j, k))], lbl[LOW.index((j, k))]
-
-    away = 1 - yh
-    c_yh = [remote(unit(z, away, h), yr.at[h], s_yh.at[h], r_yh.at[h], at(r=r_y2)) for h in range(2)]
-
-    def z_sum(h):
-        for u in range(2):
-            c_rm[u][h].wait_recv()
-            c_rp[u][h].wait_recv()
-        ut[2 * core + away, z, halves[h], :] = (
-            ut[2 * core + away, z, halves[h], :] + (rm[away, h] + rp[away, h]))
-        c_yh[h].start()
-
-    z_sum(0)
+    parts = [split(sums[:, pl.ds(k * B, B)]) for k in range(S)]
+    for k in range(S):
+        acc = sums[:, pl.ds(k * B, B)]
+        for j in range(k + 1, S):
+            acc = acc + dot3(parts[j], low(j, k))
+        xt[k] = -acc
+    c_xa = [remote(xt.at[k], xa.at[t_own, q_own, :], s_xa.at[k], r_xa.at[t_own, z], at(r=k)) for k in range(S)]
+    c_xb = [remote(xt.at[k], xb.at[core, q_own, :], s_xb.at[k], r_xb.at[core, z], at(r=b_row, c=k)) for k in range(S)]
+
+    def b_self(k):
+        return (row == b_row) & (col == k)
+
+    for k in (3, 2, 1, 0):
+        @pl.when(jnp.logical_not(b_self(k)))
+        def _():
+            c_xb[k].start()
+
+        @pl.when(b_self(k))
+        def _():
+            xb[core, q_own, :] = xt[k]
+    for k in range(S):
+        @pl.when(row != k)
+        def _():
+            c_xa[k].start()
+
+        @pl.when(row == k)
+        def _():
+            xa[t_own, q_own, :] = xt[k]
 
     @pl.when(col < S)
     def _():
-        for k in (3, 2, 1, 0):
+        for k in range(S):
             acc = jnp.concatenate([pn[k, pl.ds(0, B), :] * zero, pn[k, pl.ds(B, B), :]], axis=0)
             for j in range(k + 1, S):
-                acc = acc - dot3((pbh[j], pbl[j]), low(j, k))
-            hi, lo = split(acc)
-            pbh[k] = hi
-            pbl[k] = lo
+                acc = acc + dot3((pbh[j], pbl[j]), low(j, k))
             hi, lo = split(acc.T)
             ph[k] = hi
             plo[k] = lo
 
-    z_sum(1)
-
     dload.wait()
 
     @pl.when((row < S) & (col < S))
     def _():
         ones = (lax.broadcasted_iota(jnp.int32, (B, B), 0) == lax.broadcasted_iota(jnp.int32, (B, B), 1))
         for m in range(S):
-            for k in range(S):
-                if m < k:
-                    mt[m, k] = jnp.zeros((B, B), F32)
-                elif m == k:
-                    mt[m, k] = ones.astype(F32)
-                else:
-                    acc = lt[LOW.index((m, k))]
-                    for j in range(k + 1, m):
-                        acc = acc + dot3(low(m, j), split(mt[j, k]))
-                    mt[m, k] = -acc
+            mt[m, m] = ones.astype(F32)
+            for k in range(m + 1, S):
+                mt[m, k] = jnp.zeros((B, B), F32)
         zo[...] = jnp.zeros((B, B), F32)
         for m in range(S):
             part = dot3(split(dv[m]), split(mt[m, col]))
             zo[...] = zo[...] + dot3(split(mt[m, row].T), split(part))
-
-    for h in range(2):
-        c_yh[h].wait_recv()
-    total = ut[2 * core + yh, z] + jnp.concatenate([rm[yh, h] + rp[yh, h] + yr[h] for h in range(2)], axis=0)
-    found = {}
-    for k in (3, 2, 1, 0):
-        acc = total[:, k * B:(k + 1) * B]
-        for j in range(k + 1, S):
-            acc = acc + dot3(found[j], low(j, k))
-        xt[k] = -acc
-        found[k] = split(-acc)
-    c_xa = [remote(xt.at[k], xa.at[t_own, q_own, :], s_xa.at[k], r_xa.at[t_own, z], at(r=k)) for k in range(S)]
-    c_xb = [remote(xt.at[k], xb.at[core, q_own, :], s_xb.at[k], r_xb.at[core, z], at(r=b_row, c=k)) for k in range(S)]
-
-    def b_self(k):
-        return (row == b_row) & (col == k)
-
-    for k in (3, 2, 1, 0):
-        @pl.when(jnp.logical_not(b_self(k)))
-        def _():
-            c_xb[k].start()
-
-        @pl.when(b_self(k))
-        def _():
-            xb[core, q_own, :] = xt[k]
-    for k in range(S):
-        @pl.when(row != k)
-        def _():
-            c_xa[k].start()
-
-        @pl.when(row == k)
-        def _():
-            xa[t_own, q_own, :] = xt[k]
 
     c_zc = remote(zp.at[1 - core], zc, s_zc, r_zc, at(r=r_core))
     c_zd = [remote(zp.at[core, :, pl.ds(((quad + d) % 8) * 32, 32), :], zr.at[d - 1], s_zd.at[d - 1], r_zd.at[d - 1],
@@ -565,7 +590,9 @@
                 @pl.when(cond)
                 def _():
                     copy.wait_send()
-    for copy in [core_copy(k) for k in range(S)] + c_op + c_om + c_rm[0] + c_rm[1] + c_rp[0] + c_rp[1] + c_yh:
+    for copy in [core_copy(k) for k in range(S)] + [y_copy(k) for k in range(4)] + [c_op, c_om, c_yh, e_op, e_om]:
+        copy.wait_send()
+    for copy in c_rm + c_rp + e_rm + e_rp:
         copy.wait_send()
 
     for k in range(S):
@@ -604,7 +631,8 @@
         vmem(4, B, 2 * B, kind=BF16), vmem(4, B, 2 * B, kind=BF16),
         vmem(6, B, B), vmem(6, B, B, kind=BF16), vmem(6, B, B, kind=BF16),
         vmem(4, 4, 64, wide), vmem(2, 4, 64, wide),
-        vmem(2, 32, wide), vmem(2, 32, wide), vmem(2, 2, 32, wide), vmem(2, 2, 32, wide), vmem(2, 32, wide),
+        vmem(32, wide), vmem(32, wide), vmem(2, 32, wide), vmem(2, 32, wide), vmem(32, wide),
+        vmem(4, 32, wide), vmem(16, wide), vmem(16, wide), vmem(2, 16, wide), vmem(2, 16, wide), vmem(64, wide),
         vmem(4, 64, B), vmem(4, B, B), vmem(2, B, B), vmem(4, B, B),
         vmem(2 * B, B, kind=BF16), vmem(2 * B, B, kind=BF16),
         vmem(2, 2, B, B), vmem(2, B, B), vmem(7, 2, 32, B), vmem(2, 32, B), vmem(B, B),
@@ -612,7 +640,8 @@
         dma((2, 4)), dma((2,)), dma, dma((2, 4)), dma((7,)),
         dma((7,)), dma((7,)), dma((6,)), dma((6,)), dma((8,)), dma((8,)),
         dma((6, 4)), dma((6,)), dma((4,)), dma((4,)),
-        dma((2, 2)), dma((2, 2)), dma((2, 2, 2)), dma((2, 2, 2)), dma((2,)), dma((2,)),
+        dma((2,)), dma((2,)), dma((2, 2)), dma((2, 2)), dma, dma,
+        dma((4,)), dma((4,)), dma((2,)), dma((2,)), dma((2, 2)), dma((2, 2)),
         dma((4,)), dma((4, 4)), dma((4,)), dma((2, 4)),
         dma, dma, dma((7,)), dma((7,)), dma((2,)), dma((8,)),
     ]

time: 94.6 us -> 91.9 us (0.971)
  Pallas kernels: 89.6 us -> 87.6 us
    pallas_call x1, Pallas kernels: 89.6 us -> 87.6 us  [body(): pl.pallas_call(kernel, out_shape=jax.ShapeDtypeStruct(prior.shape, F32),...]
where the time goes in v5:
time: 91.9 us; the launch traced here: 90.9 us
  Pallas kernels  87.6 us (95%)
  local copies, waits for them, and re-layouts  3.27 us (4%)
    pallas_call x1, Pallas kernels, body(): pl.pallas_call(kernel, out_shape=jax.ShapeDtypeStruct(prior.shape, F32),...  87.6 us
    unnamed x1, local copies, waits for them, and re-layouts  3.27 us

profile of v5, /device:TPU:32, one launch (start us, length us, event | category | flops | bytes accessed | tf_op | source)
XLA Modules:
  0.0 90.9 jit_solution(3655327526108520456)
XLA Ops:
  0.0 87.6 %shard_map.46 = f32[2,256,4,256]{3,2,1,0:T(4,128)} custom-call(f32[2,256,4,256]{3,2,1,0:T(4,128)} %prior.1, f32[2,256,4,256]{3,2,1,0:T(4,128)} %lfac.1, s32[32,32]{1,0:T(8,128)} %tile_mask.1, f32[4,256,256]{2,1,0:T(8,128)} %dinv.1), custom_call_target="tpu_custom_call" | custom-call | tf_op jit(solution)/shard_map/pallas_call | solution.py:648
  87.6 3.3 %copy.6 = f32[2,256,4,256]{3,2,1,0:T(4,128)} copy(f32[2,256,4,256]{3,2,1,0:T(4,128)} %shard_map.46) | data formatting | bytes 4194304

commit v6 on v5

--- a/solution.py
+++ b/solution.py
@@ -11,6 +11,9 @@
 BF16 = jnp.bfloat16
 MESH = pl.DeviceIdType.MESH
 LOW = [(1, 0), (2, 0), (2, 1), (3, 0), (3, 1), (3, 2)]
+LATE = 32
+TOP = 64 - LATE
+HALF = LATE // 2
 CORE_OF = {1: 1, 2: 0, 3: 1}
 
 
@@ -332,8 +335,8 @@
     yd_recv(3)
     products(k_sd)
 
-    top, end = pl.ds(0, 32), pl.ds(32, 32)
-    low16, high16 = pl.ds(32, 16), pl.ds(48, 16)
+    top, end = pl.ds(0, TOP), pl.ds(TOP, LATE)
+    low_half, high_half = pl.ds(TOP, HALF), pl.ds(TOP + HALF, HALF)
     q_op, q_rm, q_rp = (z + 2) % 4, (z + 1) % 4, (z + 3) % 4
     away = 1 - yh
     t_away = 2 * core + away
@@ -354,12 +357,12 @@
         y_copy(q).wait_recv()
         ut[t_own, q, end, :] = ut[t_own, q, end, :] + yq[q]
 
-    e_op = remote(ut.at[t_own, q_op, low16, :], op1, s_eo.at[0], r_eo.at[0], at(r=r_zp))
-    e_om = remote(ut.at[t_own, q_op, high16, :], om1, s_eo.at[1], r_eo.at[1], at(r=r_zm))
+    e_op = remote(ut.at[t_own, q_op, low_half, :], op1, s_eo.at[0], r_eo.at[0], at(r=r_zp))
+    e_om = remote(ut.at[t_own, q_op, high_half, :], om1, s_eo.at[1], r_eo.at[1], at(r=r_zm))
     e_rm = [remote(ut.at[t_own, q_rm, part, :], rm1.at[n], s_er.at[0, n], r_er.at[0, n], at(r=r_zp))
-            for n, part in enumerate((low16, high16))]
+            for n, part in enumerate((low_half, high_half))]
     e_rp = [remote(ut.at[t_own, q_rp, part, :], rp1.at[n], s_er.at[1, n], r_er.at[1, n], at(r=r_zm))
-            for n, part in enumerate((low16, high16))]
+            for n, part in enumerate((low_half, high_half))]
 
     def core_add(q):
         for u in range(2):
@@ -396,10 +399,10 @@
     l_step(l_order[3], later, (2, 3))
     l_step(0, place == 3, (1,))
     e_op.wait_recv()
-    ut[t_own, q_rm, low16, :] = ut[t_own, q_rm, low16, :] + op1[...]
+    ut[t_own, q_rm, low_half, :] = ut[t_own, q_rm, low_half, :] + op1[...]
     e_rm[0].start()
     e_om.wait_recv()
-    ut[t_own, q_rp, high16, :] = ut[t_own, q_rp, high16, :] + om1[...]
+    ut[t_own, q_rp, high_half, :] = ut[t_own, q_rp, high_half, :] + om1[...]
     e_rp[1].start()
     for u in range(2):
         c_rm[u].wait_recv()
@@ -414,9 +417,9 @@
     for n in range(2):
         e_rm[n].wait_recv()
         e_rp[n].wait_recv()
-    sums[pl.ds(32, 32), :] = ut[t_own, z, end, :] + jnp.concatenate([rm1[n] + rp1[n] for n in range(2)], axis=0)
+    sums[end, :] = ut[t_own, z, end, :] + jnp.concatenate([rm1[n] + rp1[n] for n in range(2)], axis=0)
     c_yh.wait_recv()
-    sums[pl.ds(0, 32), :] = ut[t_own, z, top, :] + (rm[yh] + rp[yh] + yr[...])
+    sums[top, :] = ut[t_own, z, top, :] + (rm[yh] + rp[yh] + yr[...])
 
     for u, (j, k) in enumerate(LOW):
         @pl.when(core != CORE_OF[j])
@@ -437,18 +440,18 @@
         lbl[u] = lo
 
     parts = [split(sums[:, pl.ds(k * B, B)]) for k in range(S)]
-    for k in range(S):
+    c_xa = [remote(xt.at[k], xa.at[t_own, q_own, :], s_xa.at[k], r_xa.at[t_own, z], at(r=k)) for k in range(S)]
+    c_xb = [remote(xt.at[k], xb.at[core, q_own, :], s_xb.at[k], r_xb.at[core, z], at(r=b_row, c=k)) for k in range(S)]
+
+    def b_self(k):
+        return (row == b_row) & (col == k)
+
+    for k in (3, 2, 1, 0):
         acc = sums[:, pl.ds(k * B, B)]
         for j in range(k + 1, S):
             acc = acc + dot3(parts[j], low(j, k))
         xt[k] = -acc
-    c_xa = [remote(xt.at[k], xa.at[t_own, q_own, :], s_xa.at[k], r_xa.at[t_own, z], at(r=k)) for k in range(S)]
-    c_xb = [remote(xt.at[k], xb.at[core, q_own, :], s_xb.at[k], r_xb.at[core, z], at(r=b_row, c=k)) for k in range(S)]
-
-    def b_self(k):
-        return (row == b_row) & (col == k)
-
-    for k in (3, 2, 1, 0):
+
         @pl.when(jnp.logical_not(b_self(k)))
         def _():
             c_xb[k].start()
@@ -489,9 +492,9 @@
             part = dot3(split(dv[m]), split(mt[m, col]))
             zo[...] = zo[...] + dot3(split(mt[m, row].T), split(part))
 
-    c_zc = remote(zp.at[1 - core], zc, s_zc, r_zc, at(r=r_core))
-    c_zd = [remote(zp.at[core, :, pl.ds(((quad + d) % 8) * 32, 32), :], zr.at[d - 1], s_zd.at[d - 1], r_zd.at[d - 1],
-                   at(r=((quad + d) % 8) * 2 + core)) for d in range(1, 8)]
+    c_zc = [remote(zp.at[1 - core, m], zc.at[m], s_zc.at[m], r_zc.at[m], at(r=r_core)) for m in range(2)]
+    c_zd = [[remote(zp.at[core, m, pl.ds(((quad + d) % 8) * 32, 32), :], zr.at[d - 1, m], s_zd.at[d - 1, m],
+                    r_zd.at[d - 1, m], at(r=((quad + d) % 8) * 2 + core)) for d in range(1, 8)] for m in range(2)]
     c_zf = [remote(zs.at[m], zf.at[pl.ds(quad * 32, 32), :], s_zf.at[m], r_zf.at[quad], at(r=2 * m + core))
             for m in range(2)]
 
@@ -502,10 +505,8 @@
     cols_new = [((col < S) & (row >= S), w_col[0]), (col < S, w_col[1])]
     writes = rows_new + cols_new + [((row < S) & (col < S), w_dia)]
 
-    def diagonal(side):
-        @pl.loop(0, 2)
-        def _(m):
-            zp[side, m] = dot3((ph[2 * m + side], plo[2 * m + side]), (xh[...], xl[...]))
+    def diagonal(side, m):
+        zp[side, m] = dot3((ph[2 * m + side], plo[2 * m + side]), (xh[...], xl[...]))
 
     @pl.when(col < S)
     def _():
@@ -517,23 +518,26 @@
             hi, lo = split(xb[a])
             xh[pl.ds(a * B, B), :] = hi
             xl[pl.ds(a * B, B), :] = lo
-        diagonal(1 - core)
-        c_zc.start()
-        diagonal(core)
+        for m in range(2):
+            diagonal(1 - core, m)
+            c_zc[m].start()
+        for m in range(2):
+            diagonal(core, m)
+            c_zc[m].wait_recv()
+            zp[core, m] = zp[core, m] + zc[m]
+            for copy in c_zd[m]:
+                copy.start()
         for cond, copy in cols_new:
             @pl.when(cond)
             def _():
                 copy.start()
-        c_zc.wait_recv()
-        zp[core] = zp[core] + zc[...]
-        for copy in c_zd:
-            copy.start()
-        acc = zp[core, :, pl.ds(quad * 32, 32), :]
-        for d in range(7):
-            c_zd[d].wait_recv()
-            acc = acc + zr[d]
-        zs[...] = acc
         for m in range(2):
+            acc = zp[core, m, pl.ds(quad * 32, 32), :]
+            for d in range(7):
+                c_zd[m][d].wait_recv()
+                acc = acc + zr[d, m]
+            zs[m] = acc
+
             @pl.when(quad != m)
             def _():
                 c_zf[m].start()
@@ -606,8 +610,7 @@
 
     @pl.when(col < S)
     def _():
-        c_zc.wait_send()
-        for copy in c_zd:
+        for copy in c_zc + c_zd[0] + c_zd[1]:
             copy.wait_send()
         for m in range(2):
             @pl.when(quad != m)
@@ -631,8 +634,9 @@
         vmem(4, B, 2 * B, kind=BF16), vmem(4, B, 2 * B, kind=BF16),
         vmem(6, B, B), vmem(6, B, B, kind=BF16), vmem(6, B, B, kind=BF16),
         vmem(4, 4, 64, wide), vmem(2, 4, 64, wide),
-        vmem(32, wide), vmem(32, wide), vmem(2, 32, wide), vmem(2, 32, wide), vmem(32, wide),
-        vmem(4, 32, wide), vmem(16, wide), vmem(16, wide), vmem(2, 16, wide), vmem(2, 16, wide), vmem(64, wide),
+        vmem(TOP, wide), vmem(TOP, wide), vmem(2, TOP, wide), vmem(2, TOP, wide), vmem(TOP, wide),
+        vmem(4, LATE, wide), vmem(HALF, wide), vmem(HALF, wide), vmem(2, HALF, wide), vmem(2, HALF, wide),
+        vmem(64, wide),
         vmem(4, 64, B), vmem(4, B, B), vmem(2, B, B), vmem(4, B, B),
         vmem(2 * B, B, kind=BF16), vmem(2 * B, B, kind=BF16),
         vmem(2, 2, B, B), vmem(2, B, B), vmem(7, 2, 32, B), vmem(2, 32, B), vmem(B, B),
@@ -643,7 +647,7 @@
         dma((2,)), dma((2,)), dma((2, 2)), dma((2, 2)), dma, dma,
         dma((4,)), dma((4,)), dma((2,)), dma((2,)), dma((2, 2)), dma((2, 2)),
         dma((4,)), dma((4, 4)), dma((4,)), dma((2, 4)),
-        dma, dma, dma((7,)), dma((7,)), dma((2,)), dma((8,)),
+        dma((2,)), dma((2,)), dma((7, 2)), dma((7, 2)), dma((2,)), dma((8,)),
     ]
     return pl.pallas_call(
         kernel,

time: 91.9 us -> 91.2 us (level)
  no operation moved by 1% of the time
where the time goes in v6:
time: 91.2 us; the launch traced here: 91.1 us
  Pallas kernels  87.8 us (96%)
  local copies, waits for them, and re-layouts  3.27 us (4%)
    pallas_call x1, Pallas kernels, body(): pl.pallas_call(kernel, out_shape=jax.ShapeDtypeStruct(prior.shape, F32),...  87.8 us
    unnamed x1, local copies, waits for them, and re-layouts  3.27 us

profile of v6, /device:TPU:32, one launch (start us, length us, event | category | flops | bytes accessed | tf_op | source)
XLA Modules:
  0.0 91.1 jit_solution(12468860165571117685)
XLA Ops:
  0.0 87.8 %shard_map.46 = f32[2,256,4,256]{3,2,1,0:T(4,128)} custom-call(f32[2,256,4,256]{3,2,1,0:T(4,128)} %prior.1, f32[2,256,4,256]{3,2,1,0:T(4,128)} %lfac.1, s32[32,32]{1,0:T(8,128)} %tile_mask.1, f32[4,256,256]{2,1,0:T(8,128)} %dinv.1), custom_call_target="tpu_custom_call" | custom-call | tf_op jit(solution)/shard_map/pallas_call | solution.py:652
  87.8 3.3 %copy.6 = f32[2,256,4,256]{3,2,1,0:T(4,128)} copy(f32[2,256,4,256]{3,2,1,0:T(4,128)} %shard_map.46) | data formatting | bytes 4194304

commit v7 on v6

--- a/solution.py
+++ b/solution.py
@@ -311,10 +311,10 @@
         l_step(k_sd, None)
         x_recv(3)
         d_y(3)
+    products(k_s)
     l_step(l_order[1], early, (2, 3))
     l_step(l_order[2], early, (2, 3))
     l_step(l_order[0], later, (2, 3))
-    products(k_s)
 
     @pl.when(inner)
     def _():
@@ -371,9 +371,9 @@
     for k in range(S):
         core_copy(k).wait_recv()
     core_add(q_op)
+    y_copy(q_op).start()
     c_op.start()
     c_om.start()
-    y_copy(q_op).start()
     core_add(q_rm)
     c_rm[1].start()
     y_copy(q_rm).start()

time: 91.2 us -> 90.8 us (level)
  no operation moved by 1% of the time
where the time goes in v7:
time: 90.8 us; the launch traced here: 90.6 us
  Pallas kernels  87.3 us (96%)
  local copies, waits for them, and re-layouts  3.27 us (4%)
    pallas_call x1, Pallas kernels, body(): pl.pallas_call(kernel, out_shape=jax.ShapeDtypeStruct(prior.shape, F32),...  87.3 us
    unnamed x1, local copies, waits for them, and re-layouts  3.27 us

profile of v7, /device:TPU:32, one launch (start us, length us, event | category | flops | bytes accessed | tf_op | source)
XLA Modules:
  0.0 90.6 jit_solution(879454243754476683)
XLA Ops:
  0.0 87.3 %shard_map.46 = f32[2,256,4,256]{3,2,1,0:T(4,128)} custom-call(f32[2,256,4,256]{3,2,1,0:T(4,128)} %prior.1, f32[2,256,4,256]{3,2,1,0:T(4,128)} %lfac.1, s32[32,32]{1,0:T(8,128)} %tile_mask.1, f32[4,256,256]{2,1,0:T(8,128)} %dinv.1), custom_call_target="tpu_custom_call" | custom-call | tf_op jit(solution)/shard_map/pallas_call | solution.py:652
  87.3 3.3 %copy.6 = f32[2,256,4,256]{3,2,1,0:T(4,128)} copy(f32[2,256,4,256]{3,2,1,0:T(4,128)} %shard_map.46) | data formatting | bytes 4194304

commit v8 on v7

--- a/solution.py
+++ b/solution.py
@@ -321,19 +321,19 @@
         for ch in (2, 3):
             quarter(k_pd, ch, s_out.at[3 + ch], r_out.at[3 + ch], to_o).wait_recv()
     products(k_pd)
+
+    @pl.when(source)
+    def _():
+        xd_recv(2)
+
+    @pl.when(inner)
+    def _():
+        yd_recv(2)
+    yd_recv(3)
+    products(k_sd)
     l_step(l_order[3], early, (2, 3))
     l_step(l_order[1], later, (2, 3))
     l_step(0, row == 9, (1,))
-
-    @pl.when(source)
-    def _():
-        xd_recv(2)
-
-    @pl.when(inner)
-    def _():
-        yd_recv(2)
-    yd_recv(3)
-    products(k_sd)
 
     top, end = pl.ds(0, TOP), pl.ds(TOP, LATE)
     low_half, high_half = pl.ds(TOP, HALF), pl.ds(TOP + HALF, HALF)

time: 90.8 us -> 89.4 us (0.985)
  Pallas kernels: 87.3 us -> 86 us
    pallas_call x1, Pallas kernels: 87.3 us -> 86 us  [body(): pl.pallas_call(kernel, out_shape=jax.ShapeDtypeStruct(prior.shape, F32),...]
where the time goes in v8:
time: 89.4 us; the launch traced here: 89.3 us
  Pallas kernels  86 us (96%)
  local copies, waits for them, and re-layouts  3.27 us (4%)
    pallas_call x1, Pallas kernels, body(): pl.pallas_call(kernel, out_shape=jax.ShapeDtypeStruct(prior.shape, F32),...  86 us
    unnamed x1, local copies, waits for them, and re-layouts  3.27 us

profile of v8, /device:TPU:32, one launch (start us, length us, event | category | flops | bytes accessed | tf_op | source)
XLA Modules:
  0.0 89.3 jit_solution(3191114091966900135)
XLA Ops:
  0.0 86.0 %shard_map.46 = f32[2,256,4,256]{3,2,1,0:T(4,128)} custom-call(f32[2,256,4,256]{3,2,1,0:T(4,128)} %prior.1, f32[2,256,4,256]{3,2,1,0:T(4,128)} %lfac.1, s32[32,32]{1,0:T(8,128)} %tile_mask.1, f32[4,256,256]{2,1,0:T(8,128)} %dinv.1), custom_call_target="tpu_custom_call" | custom-call | tf_op jit(solution)/shard_map/pallas_call | solution.py:652
  86.0 3.3 %copy.6 = f32[2,256,4,256]{3,2,1,0:T(4,128)} copy(f32[2,256,4,256]{3,2,1,0:T(4,128)} %shard_map.46) | data formatting | bytes 4194304
